TPU v7x, 256 devices: a whole 4x4x8 slice. The times are simulated.
256 devices in a mesh: blk: 128 (over x, y, z), ch: 2 (over core).
Axes of the slice: x: 4, y: 4, z: 8, core: 2. Of those that a mesh axis runs over, the one named last changes fastest.
Arguments:
- raw: float32 [2048, 8, 2, 4096], P('blk', 'ch'), may hold values from -6 to 6
- range_filter: float32 [2, 4096], replicated, may hold values from -6 to 6
- recon: float32 [2, 8, 2048], replicated, may hold values from -5 to 5
- rcmc_coef: float32 [8, 2048], replicated, may hold values from -6 to 6
- band_offset: int32 [4096], P(('blk', 'ch')), may hold values from -8 to 7, as said below
- band_width: int32 [4096], P(('blk', 'ch')), may hold values from 1 to 8
- az_filter: float32 [2, 2048, 4096], P(None, None, ('blk', 'ch')), may hold values from -6 to 6
Outputs:
- image: float32 [2, 2048, 4096], P(None, None, ('blk', 'ch'))
Inputs may be any that keep to these rules, and one draw needn't show every extreme that they name: band_offset + band_width <= 8 for every bin.
All inputs are finite; a program needn't handle non-finite values.
Results may differ from a plain program's by a relative error of at most 0.0001.
Values sent between devices are 32-bit elements; how exact they have to be, the bound alone decides.
No kernel may reach another device: no remote copies, remote signals or barrier semaphores. Data moves between devices by JAX's collectives and lax.ppermute only.
A program may use at most 128 MiB of HBM per device.

v0:
```python
import math

import jax
import jax.numpy as jnp
from jax import lax
from jax.sharding import PartitionSpec as P

REACH = 8


HIGHEST_MODE = lax.Precision.HIGHEST


def with_halo(block, sides, width):
    for axis, dim in sides:
        count = lax.axis_size(axis)
        forward = [(i, i + 1) for i in range(count - 1)]
        backward = [(target, source) for source, target in forward]
        low = lax.ppermute(
            lax.slice_in_dim(block, block.shape[dim] - width, None, axis=dim), axis, forward
        )
        high = lax.ppermute(lax.slice_in_dim(block, 0, width, axis=dim), axis, backward)
        block = jnp.concatenate([low, block, high], axis=dim)
    return block


def dft_table(length, direction):
    counter = jnp.arange(length, dtype=jnp.int32)
    products = counter[:, None] * counter[None, :] % length
    phases = direction * 2.0 * math.pi / length * products.astype(jnp.float32)
    return (jnp.cos(phases), jnp.sin(phases))


def twiddle_table(first_len, second_len, direction):
    exponent = (
        jnp.arange(first_len, dtype=jnp.int32)[:, None]
        * jnp.arange(second_len, dtype=jnp.int32)[None, :]
    )
    phases = direction * 2.0 * math.pi / (first_len * second_len) * exponent.astype(jnp.float32)
    return (jnp.cos(phases), jnp.sin(phases))


def factor_pair(length):
    first_len = 2 ** ((length.bit_length() - 1) // 2)
    return (first_len, length // first_len)


def complex_dot(left_form, right_form, output_form, left_re, left_im, right_re, right_im):
    joined = "p" + left_form + ",po" + right_form + "->o" + output_form
    stacked = jnp.stack([left_re, left_im], 0)
    blocks = jnp.stack([jnp.stack([right_re, right_im], 0), jnp.stack([-right_im, right_re], 0)], 0)
    result = jnp.einsum(joined, stacked, blocks, precision=HIGHEST_MODE)
    return (result[0], result[1])


def dft_last(real_part, imag_part, direction):
    length = real_part.shape[-1]
    first_len, second_len = factor_pair(length)
    leading = real_part.shape[:-1]
    split_re = real_part.reshape(leading + (first_len, second_len))
    split_im = imag_part.reshape(leading + (first_len, second_len))
    table_re, table_im = dft_table(first_len, direction)
    section_re, section_im = complex_dot(
        "...nq", "kn", "...kq", split_re, split_im, table_re, table_im
    )
    twist_re, twist_im = twiddle_table(first_len, second_len, direction)
    section_re, section_im = (
        section_re * twist_re - section_im * twist_im,
        section_re * twist_im + section_im * twist_re,
    )
    table_re, table_im = dft_table(second_len, direction)
    final_re, final_im = complex_dot(
        "...kq", "jq", "...kj", section_re, section_im, table_re, table_im
    )
    final_re = jnp.swapaxes(final_re, -1, -2).reshape(leading + (length,))
    final_im = jnp.swapaxes(final_im, -1, -2).reshape(leading + (length,))
    return (final_re, final_im)


def dft_first(real_part, imag_part, direction):
    length = real_part.shape[0]
    trailing = real_part.shape[1:]
    first_len, second_len = factor_pair(length)
    split_re = real_part.reshape((first_len, second_len) + trailing)
    split_im = imag_part.reshape((first_len, second_len) + trailing)
    table_re, table_im = dft_table(first_len, direction)
    section_re, section_im = complex_dot(
        "nq...", "kn", "kq...", split_re, split_im, table_re, table_im
    )
    twist_re, twist_im = twiddle_table(first_len, second_len, direction)
    twist_re = twist_re.reshape((first_len, second_len) + (1,) * len(trailing))
    twist_im = twist_im.reshape((first_len, second_len) + (1,) * len(trailing))
    section_re, section_im = (
        section_re * twist_re - section_im * twist_im,
        section_re * twist_im + section_im * twist_re,
    )
    table_re, table_im = dft_table(second_len, direction)
    final_re, final_im = complex_dot(
        "kq...", "jq", "kj...", section_re, section_im, table_re, table_im
    )
    final_re = jnp.swapaxes(final_re, 0, 1).reshape((length,) + trailing)
    final_im = jnp.swapaxes(final_im, 0, 1).reshape((length,) + trailing)
    return (final_re, final_im)


def channel_mix(turned, weights):
    doppler_re, doppler_im = dft_first(turned[:, :, 0, :], turned[:, :, 1, :], -1.0)
    mixed_re, mixed_im = complex_dot(
        "fcr", "cf", "fr", doppler_re, doppler_im, weights[0], weights[1]
    )
    return jnp.stack([mixed_re, mixed_im], 1)


def local_weights(recon, count):
    return lax.dynamic_slice_in_dim(recon, lax.axis_index("ch") * count, count, 1)


def migrate(window, band_offset, band_width, rcmc_coef):
    owned = band_offset.shape[0]
    span = window.shape[2]
    source = jnp.arange(span, dtype=jnp.int32)[None, :, None]
    tap_index = jnp.arange(REACH, dtype=jnp.int32)[:, None, None]
    target = (
        jnp.arange(owned, dtype=jnp.int32)[None, None, :]
        + REACH
        + band_offset[None, None, :]
        + tap_index
    )
    select = ((source == target) & (tap_index < band_width[None, None, :])).astype(jnp.float32)
    gathered_re = jnp.einsum("fs,ksj->fkj", window[:, 0, :], select, precision=HIGHEST_MODE)
    gathered_im = jnp.einsum("fs,ksj->fkj", window[:, 1, :], select, precision=HIGHEST_MODE)
    moved_re = jnp.einsum("fkj,kf->fj", gathered_re, rcmc_coef, precision=HIGHEST_MODE)
    moved_im = jnp.einsum("fkj,kf->fj", gathered_im, rcmc_coef, precision=HIGHEST_MODE)
    return (moved_re, moved_im)


def body(raw, range_filter, recon, rcmc_coef, band_offset, band_width, az_filter):
    spectrum_re, spectrum_im = dft_last(raw[:, :, 0, :], raw[:, :, 1, :], -1.0)
    shaped_re = spectrum_re * range_filter[0] - spectrum_im * range_filter[1]
    shaped_im = spectrum_re * range_filter[1] + spectrum_im * range_filter[0]
    back_re, back_im = dft_last(shaped_re, shaped_im, 1.0)
    samples = raw.shape[3]
    compressed = jnp.stack([back_re / samples, back_im / samples], 2)
    turned = lax.all_to_all(compressed, "blk", split_axis=3, concat_axis=0, tiled=True)
    partial_mix = channel_mix(turned, local_weights(recon, turned.shape[1]))
    total = lax.psum(partial_mix, "ch")
    owned = total.shape[2] // lax.axis_size("ch")
    share = lax.dynamic_slice_in_dim(total, lax.axis_index("ch") * owned, owned, 2)
    window = with_halo(share, ((("blk", "ch"), 2),), REACH)
    moved_re, moved_im = migrate(window, band_offset, band_width, rcmc_coef)
    focus_re = moved_re * az_filter[0] - moved_im * az_filter[1]
    focus_im = moved_re * az_filter[1] + moved_im * az_filter[0]
    image_re, image_im = dft_first(focus_re, focus_im, 1.0)
    lines = window.shape[0]
    return jnp.stack([image_re / lines, image_im / lines], 0)


def solution(mesh):
    return jax.shard_map(
        body,
        mesh=mesh,
        in_specs=(
            P("blk", "ch", None, None),
            P(),
            P(),
            P(),
            P(("blk", "ch")),
            P(("blk", "ch")),
            P(None, None, ("blk", "ch")),
        ),
        out_specs=P(None, None, ("blk", "ch")),
        check_vma=False,
    )
```

profile of v0, /device:TPU:2, one launch (start us, length us, event | category | flops | bytes accessed | tf_op | source)
XLA Modules:
  0.0 361.1 jit_solution(4716521601934782624)
XLA Ops:
  7.4 9.5 %slice_reduce_fusion.1 = (f32[16,4,4096]{2,1,0:T(4,128)}, f32[16,4,4096]{2,1,0:T(4,128)S(1)}) fusion(f32[16,4,2,4096]{3,2,1,0:T(2,128)} %param.7), kind=kLoop, calls=%fused_computation.54 | loop fusion | bytes 4194304 | tf_op jit(solution)/shard_map/slice | solution.py:138
  21.8 5.4 %fusion.18 = f32[2,16,4,64,64]{4,3,2,1,0:T(8,128)S(1)} fusion(f32[1,2,64,64]{3,2,0,1:T(8,128)S(1)} %get-tuple-element.42, f32[1,2,64,64]{3,2,0,1:T(8,128)S(1)} %get-tuple-element.41, f32[1,16,4,64,64]{4,3,2,1,0:T(8,128)} %reshape.481, f32[1,16,4,64,64]{4,3,2,1,0:T(8,128)S(1)} %reshape.480), kind=kOutput, calls=%fused_computation.25 | convolution fusion | flops 805847040 | bytes 4259840 | tf_op jit(solution)/shard_map/p...nq,pokn->o...kq/dot_general | solution.py:52
  28.1 6.2 %fusion.21 = f32[2,16,4,64,64]{3,4,2,1,0:T(8,128)S(1)} fusion(f32[1,2,64,64]{3,2,0,1:T(8,128)S(1)} %get-tuple-element.42, f32[1,2,64,64]{3,2,0,1:T(8,128)S(1)} %get-tuple-element.41, f32[1,16,4,64,64]{4,3,2,1,0:T(8,128)S(1)} %get-tuple-element.18, f32[1,16,4,64,64]{4,3,2,1,0:T(8,128)S(1)} %get-tuple-element.17), kind=kOutput, calls=%fused_computation.26 | convolution fusion | flops 805847040 | bytes 4259840 | tf_op jit(solution)/shard_map/p...kq,pojq->o...kj/dot_general | solution.py:52
  35.4 4.2 %fusion.24 = f32[2,16,4,64,64]{4,3,2,1,0:T(8,128)S(1)} fusion(f32[2,2,64,64,1,1]{3,2,1,0,5,4:T(8,128)S(1)} %get-tuple-element.36, f32[1,16,4,64,64]{4,3,2,1,0:T(8,128)S(1)} %get-tuple-element.16, f32[1,16,4,64,64]{4,3,2,1,0:T(8,128)S(1)} %get-tuple-element.15), kind=kOutput, calls=%fused_computation.27 | convolution fusion | flops 805830656 | bytes 4259840 | tf_op jit(solution)/shard_map/p...nq,pokn->o...kq/dot_general | solution.py:52
  40.6 6.2 %fusion.27 = f32[2,16,4,64,64]{3,4,2,1,0:T(8,128)S(1)} fusion(f32[2,2,64,64,1,1]{3,2,1,0,5,4:T(8,128)S(1)} %get-tuple-element.36, f32[1,16,4,64,64]{4,3,2,1,0:T(8,128)S(1)} %get-tuple-element.14, f32[1,16,4,64,64]{4,3,2,1,0:T(8,128)S(1)} %get-tuple-element.13), kind=kOutput, calls=%fused_computation.28 | convolution fusion | flops 805830656 | bytes 4259840 | tf_op jit(solution)/shard_map/p...kq,pojq->o...kj/dot_general | solution.py:52
  48.8 7.9 %copy.176 = f32[16,4,64,64]{0,1,3,2:T(4,128)} copy(f32[16,4,64,64]{3,2,1,0:T(8,128)} %get-tuple-element.23) | data formatting | bytes 2097152 | tf_op jit(solution)/shard_map/div | solution.py:143
  56.7 6.1 %copy.177 = f32[16,4,64,64]{0,1,3,2:T(4,128)} copy(f32[16,4,64,64]{3,2,1,0:T(8,128)S(1)} %get-tuple-element.24) | data formatting | bytes 2097152 | tf_op jit(solution)/shard_map/div | solution.py:143
  62.8 21.3 %fusion.84 = f32[4096,4,2,16]{3,2,1,0:T(2,128)} fusion(f32[16,4,1,4096]{0,2,1,3:T(1,128)} %bitcast.232, f32[16,4,1,4096]{0,2,1,3:T(1,128)} %bitcast.231), kind=kLoop, calls=%fused_computation.164 | loop fusion | flops 524288 | bytes 4194304
  84.1 25.7 %reshape.496 = f32[128,1,4096]{2,1,0:T(1,128)} reshape(f32[4096,4,2,16]{3,2,1,0:T(2,128)} %fusion.84) | data formatting | bytes 4194304
  109.8 15.7 %all-to-all-start = ((f32[128,1,4096]{2,1,0:T(1,128)}), f32[128,1,4096]{2,1,0:T(1,128)S(1)}, u32[]{:S(2)}, u32[]{:S(2)}) async-start(f32[128,1,4096]{2,1,0:T(1,128)} %reshape.496), calls=%async_computation | async-start | bytes 4194304 | tf_op jit(solution)/shard_map/all_to_all | solution.py:144
  125.6 4.5 %copy.129 = f32[2,2,4,2048]{2,1,0,3:T(2,128)} copy(f32[2,2,4,2048]{3,2,1,0:T(4,128)S(1)} %pad_maximum_fusion.12) | data formatting | bytes 262144 | tf_op jit(solution)/shard_map/stack | solution.py:51
  130.6 46.7 %all-to-all-done = f32[128,1,4096]{2,1,0:T(1,128)S(1)} async-done(((f32[128,1,4096]{2,1,0:T(1,128)}), f32[128,1,4096]{2,1,0:T(1,128)S(1)}, u32[]{:S(2)}, u32[]{:S(2)}) %all-to-all-start) | async-done | bytes 2097184 | tf_op jit(solution)/shard_map/all_to_all | solution.py:144
  179.1 7.3 %reduce.16 = f32[128,4096]{1,0:T(8,128)S(1)} reduce(f32[128,1,4096]{2,1,0:T(1,128)} %copy-done, f32[]{:T(128)} %broadcast.639), dimensions={1}, to_apply=%all_to_all.13.reduce_sub_computation | reduce | bytes 4194308 | tf_op jit(solution)/shard_map/all_to_all | solution.py:144
  186.5 23.7 %reshape.497 = f32[4096,4,2,16]{3,2,1,0:T(2,128)} reshape(f32[128,4096]{1,0:T(8,128)S(1)} %reduce.16) | data formatting | bytes 4194304
  210.2 20.6 %copy.179 = f32[16,4,2,128,32]{4,0,3,2,1:T(8,128)} copy(f32[16,4,2,128,32]{0,2,1,4,3:T(2,128)} %bitcast.229) | data formatting | bytes 4194304 | tf_op jit(solution)/shard_map/all_to_all | solution.py:144
  230.8 7.3 %fusion.82 = (f32[2048,4,1,32]{3,0,2,1:T(8,128)}, f32[2048,4,1,32]{3,0,2,1:T(8,128)}) fusion(f32[2048,4,2,32]{3,0,2,1:T(8,128)} %bitcast.230), kind=kLoop, calls=%fused_computation.162 | loop fusion | bytes 4194304 | tf_op jit(solution)/shard_map/slice | solution.py:107
  241.6 4.5 %copy.181 = f32[1,32,64,4,32]{2,1,0,4,3:T(8,128)} copy(f32[1,32,64,4,32]{4,2,1,3,0:T(8,128)} %bitcast.233) | data formatting | bytes 2097152 | tf_op jit(solution)/shard_map/stack;reshape;squeeze | solution.py:50
  246.1 5.5 %fusion.33 = f32[2,32,64,4,32]{2,1,4,3,0:T(8,128)S(1)} fusion(f32[1,32,64,4,32]{2,1,0,4,3:T(8,128)} %copy.181, f32[1,32,64,4,32]{2,1,0,4,3:T(8,128)S(1)} %copy.180, f32[1,2,32,32]{3,2,0,1:T(8,128)S(1)} %get-tuple-element.46, f32[1,2,32,32]{3,2,0,1:T(8,128)S(1)} %get-tuple-element.45), kind=kOutput, calls=%fused_computation.30 | convolution fusion | flops 403181568 | bytes 4210688 | tf_op jit(solution)/shard_map/pnq...,pokn->okq.../dot_general | solution.py:52
  253.3 6.5 %fusion.30 = f32[2,32,64,4,32]{2,4,3,1,0:T(8,128)S(1)} fusion(f32[2,32,64,4,32]{2,1,4,3,0:T(8,128)S(1)} %pad_maximum_fusion.5, f32[1,2,64,64]{3,2,0,1:T(8,128)S(1)} %get-tuple-element.42, f32[1,2,64,64]{3,2,0,1:T(8,128)S(1)} %get-tuple-element.41), kind=kOutput, calls=%fused_computation.29 | convolution fusion | flops 805322752 | bytes 4259840 | tf_op jit(solution)/shard_map/pkq...,pojq->okj.../dot_general | solution.py:52
  272.2 4.4 %stack_reshape.15 = f32[1,2048,4,32]{1,3,2,0:T(8,128)} reshape(f32[64,32,4,32]{1,0,3,2:T(8,128)} %copy.128) | data formatting | bytes 2097152 | tf_op jit(solution)/shard_map/stack;reshape | solution.py:50
  278.1 5.9 %copy.130 = f32[2,2048,4,32]{3,2,0,1:T(4,128)} copy(f32[2,2048,4,32]{1,3,2,0:T(8,128)S(1)} %pad_maximum_fusion.6) | data formatting | bytes 4194304 | tf_op jit(solution)/shard_map/stack | solution.py:50
  283.9 23.6 %convolution_bitcast_fusion = f32[2,2048,32]{2,0,1:T(2,128)S(1)} fusion(f32[2,2,4,2048]{2,1,0,3:T(2,128)} %copy.129, f32[2,2048,4,32]{3,2,0,1:T(4,128)} %copy.130), kind=kOutput, calls=%fused_computation.48 | convolution fusion | flops 12582912 | bytes 2752512 | tf_op jit(solution)/shard_map/pfcr,pocf->ofr/dot_general | solution.py:52
  311.1 24.6 %all-reduce.2.cloned.1.call-done = f32[2048,2,32]{0,2,1:T(8,128)} async-done(((f32[2048,2,32]{0,2,1:T(8,128)}), f32[2048,2,32]{0,2,1:T(8,128)}) %all-reduce.2.cloned.1.call-update) | async-done | bytes 524304 | tf_op jit(solution)/shard_map/psum | solution.py:146
  338.9 7.7 %collective-permute-start.1 = (f32[2048,2,8]{0,2,1:T(8,128)S(1)}, f32[2048,2,8]{0,2,1:T(8,128)S(1)}, u32[]{:S(2)}, u32[]{:S(2)}) collective-permute-start(f32[2048,2,8]{0,2,1:T(8,128)S(1)} %get-tuple-element.34), channel_id=1, source_target_pairs={{1,0},{2,1},{3,2},{4,3},{5,4},{6,5},{7,6},{8,7},{9,8},{10,9},{11,1... | collective-permute-start | bytes 393224 | tf_op jit(solution)/shard_map/ppermute | solution.py:22
  (83 shorter events, 45.9 us)
Async XLA Ops:
  19.2 2.4 copy-start.4
  109.8 15.7 %copy-start.2 = (f32[2,8,2048]{2,1,0:T(8,128)S(1)}, f32[2,8,2048]{2,1,0:T(8,128)}, u32[]{:S(2)}) copy-start(f32[2,8,2048]{2,1,0:T(8,128)} %param.9) | copy-start | bytes 393220
  109.8 67.5 %all-to-all-start = ((f32[128,1,4096]{2,1,0:T(1,128)}), f32[128,1,4096]{2,1,0:T(1,128)S(1)}, u32[]{:S(2)}, u32[]{:S(2)}) async-start(f32[128,1,4096]{2,1,0:T(1,128)} %reshape.496), calls=%async_computation | async-start | bytes 4194304 | tf_op jit(solution)/shard_map/all_to_all | solution.py:144
  125.4 210.3 %all-reduce.2.cloned.1.call-start = ((), (), s32[]{:S(2)}) async-start(), calls=%async_computation.1 | async-start | bytes 1048576 | tf_op jit(solution)/shard_map/psum | solution.py:146
  125.6 4.9 %copy-start.5 = (s32[16]{0:T(128)S(1)}, s32[16]{0:T(128)}, u32[]{:S(2)}) copy-start(s32[16]{0:T(128)} %param.11) | copy-start | bytes 196
  125.6 5.0 %copy-start.6 = (s32[16]{0:T(128)S(1)}, s32[16]{0:T(128)}, u32[]{:S(2)}) copy-start(s32[16]{0:T(128)} %param.12) | copy-start | bytes 196
  177.3 1.3 copy-start
  336.7 10.9 %collective-permute-start = (f32[2048,2,8]{0,2,1:T(8,128)S(1)}, f32[2048,2,8]{0,2,1:T(8,128)S(1)}, u32[]{:S(2)}, u32[]{:S(2)}) collective-permute-start(f32[2048,2,8]{0,2,1:T(8,128)S(1)} %get-tuple-element.33), channel_id=1, source_target_pairs={{0,1},{1,2},{2,3},{3,4},{4,5},{5,6},{6,7},{7,8},{8,9},{9,10},{10,1... | collective-permute-start | bytes 393224 | tf_op jit(solution)/shard_map/ppermute | solution.py:19
  338.9 11.4 %copy-start.3 = (f32[8,2048]{1,0:T(8,128)S(1)}, f32[8,2048]{1,0:T(8,128)}, u32[]{:S(2)}) copy-start(f32[8,2048]{1,0:T(8,128)} %param.10) | copy-start | bytes 196612
  338.9 10.2 %collective-permute-start.1 = (f32[2048,2,8]{0,2,1:T(8,128)S(1)}, f32[2048,2,8]{0,2,1:T(8,128)S(1)}, u32[]{:S(2)}, u32[]{:S(2)}) collective-permute-start(f32[2048,2,8]{0,2,1:T(8,128)S(1)} %get-tuple-element.34), channel_id=1, source_target_pairs={{1,0},{2,1},{3,2},{4,3},{5,4},{6,5},{7,6},{8,7},{9,8},{10,9},{11,1... | collective-permute-start | bytes 393224 | tf_op jit(solution)/shard_map/ppermute | solution.py:22
  349.8 1.0 copy-start.1
Sparse Core Ops, SparseCore 0:
  311.1 24.6 all-reduce.1
where the time goes:
time: 367 us; the launch traced here: 361 us
  local copies, waits for them, and re-layouts  148 us (40%)
  waiting for transfers between devices  72.8 us (20%)
  matrix products  60.1 us (16%)
  other arithmetic  40.1 us (11%)
  starting transfers between devices  25.6 us (7%)
  between operations  14.1 us (4%)
    dot_general x9, matrix products, complex_dot(): result = jnp.einsum(joined, stacked, blocks, precision=HIGHEST_MODE)  59 us
    unnamed x16, local copies, waits for them, and re-layouts  50.9 us
    all_to_all x1, waiting for transfers between devices, body(): lax.all_to_all(compressed, 'blk', split_axis=3, concat_axis=0, tiled=True)  46.7 us
    another operation x9, local copies, waits for them, and re-layouts, complex_dot(): stacked = jnp.stack([left_re, left_im], 0)  26.8 us
    psum x1, waiting for transfers between devices, body(): total = lax.psum(partial_mix, 'ch')  24.6 us
    unnamed x1, other arithmetic  21.3 us
    all_to_all x2, local copies, waits for them, and re-layouts, body(): lax.all_to_all(compressed, 'blk', split_axis=3, concat_axis=0, tiled=True)  21.1 us
    all_to_all x1, starting transfers between devices, body(): lax.all_to_all(compressed, 'blk', split_axis=3, concat_axis=0, tiled=True)  15.7 us
  transfers between devices with their start and end apart: 4, of which 3 were waited for; matrix products, arithmetic and copies ran while one was open for 2% of the time, Pallas kernels for 0%

commit v1 on v0

v1 whole, which is shorter than its diff:
```python
import functools
import math

import jax
import jax.numpy as jnp
import ml_dtypes
import numpy as np
from jax import lax
from jax.experimental import pallas as pl
from jax.experimental.pallas import tpu as pltpu
from jax.sharding import PartitionSpec as P

REACH = 8
BF16 = jnp.bfloat16
F32 = jnp.float32
PARTS = (4,)
RANGE_VMEM = 60 * 2**20
CHIP = np.arange(128).reshape(4, 4, 8).transpose(0, 2, 1).reshape(128)
PLACE = np.argsort(CHIP)
TURN = ("x", "z", "y")
BLK = ("x", "y", "z")
EVERY = ("x", "y", "z", "ch")


def phase(rows, cols, length, sign):
    angle = sign * 2.0 * np.pi * ((np.outer(rows, cols) % length) / length)
    return np.cos(angle), np.sin(angle)


def pair(table):
    high = table.astype(np.float32).astype(ml_dtypes.bfloat16)
    low = (table - high.astype(np.float64)).astype(np.float32).astype(ml_dtypes.bfloat16)
    return high, low


def as_left(table):
    high, low = pair(table)
    return np.concatenate([high, high, low], axis=1)


def as_right(table):
    high, low = pair(table)
    return np.concatenate([high, high, low], axis=0)


def right_matrix(cosine, sine, scale=1.0):
    return np.block([[cosine, sine], [-sine, cosine]]) * scale


@functools.cache
def range_tables():
    t = np.arange(32)
    lane = np.arange(128)
    c32, s32 = phase(t, t, 32, -1)
    left = np.zeros((64, 32, 2))
    left[:32, :, 0], left[:32, :, 1] = c32, -s32
    left[32:, :, 0], left[32:, :, 1] = s32, c32
    first = as_left(left.reshape(64, 64))
    twist_in = np.stack(phase(t, lane, 4096, -1)).astype(np.float32)
    kl = 4 * (lane % 32) + lane // 32
    second = as_right(right_matrix(*phase(lane, kl, 128, -1)))
    third = as_right(right_matrix(*phase(kl, lane, 128, 1), scale=1.0 / 4096))
    twist_out = np.stack(phase(t, lane, 4096, 1)).astype(np.float32)
    c32, s32 = phase(t, t, 32, 1)
    wide = np.zeros((32, 2, 4, 4, 2, 32))
    for line in range(4):
        wide[:, 0, line, line, 0], wide[:, 0, line, line, 1] = c32, -s32
        wide[:, 1, line, line, 0], wide[:, 1, line, line, 1] = s32, c32
    last = as_left(wide.reshape(256, 256))
    first = np.pad(first, ((0, 0), (0, 64)))
    last = last.reshape(256, 3, 256).transpose(1, 0, 2).reshape(768, 256)
    matrices = np.concatenate([second, third, last, first], axis=0)
    return matrices, np.concatenate([twist_in, twist_out], axis=0)


@functools.cache
def line_tables():
    row = np.arange(128)
    fb = 16 * (row % 8) + row // 8
    out = []
    for j in range(16):
        source = 16 * CHIP + j
        c, s = phase(fb, source, 2048, -1)
        high, low = pair(np.block([[c, -s], [s, c]]))
        out.append(np.concatenate([high, low], axis=1))
    eye = np.eye(128).astype(ml_dtypes.bfloat16)
    return np.stack(out), np.concatenate([eye, eye], axis=1)


@functools.cache
def focus_tables():
    lane = np.arange(128)
    right = as_right(right_matrix(*phase(lane, lane, 128, 1), scale=1.0 / 2048))
    twist = np.stack(phase(np.arange(16), lane, 2048, 1)).astype(np.float32)
    return right, twist


def split(x):
    high = x.astype(BF16)
    return high, (x - high.astype(F32)).astype(BF16)


def dot(left, right):
    return jnp.dot(left, right, preferred_element_type=F32)


def left_rows(re, im):
    rh, rl = split(re)
    ih, il = split(im)
    return jnp.concatenate([rh, ih, rl, il, rh, ih], axis=1)


def right_cols(x):
    high, low = split(x)
    return jnp.concatenate([high, low, high], axis=0)


def times(ar, ai, br, bi):
    return ar * br - ai * bi, ar * bi + ai * br


def small_fft(values, sign):
    count = len(values)
    if count == 1:
        return values
    even = small_fft(values[0::2], sign)
    odd = small_fft(values[1::2], sign)
    low, high = [], []
    for k in range(count // 2):
        (er, ei), (pr, pi) = even[k], odd[k]
        if k == 0:
            tr, ti = pr, pi
        elif 4 * k == count:
            tr, ti = (-pi, pr) if sign > 0 else (pi, -pr)
        else:
            c, s = math.cos(2 * math.pi * k / count), sign * math.sin(2 * math.pi * k / count)
            tr, ti = pr * c - pi * s, pr * s + pi * c
        low.append((er + tr, ei + ti))
        high.append((er - tr, ei - ti))
    return low + high


def swap_blocks(parts):
    lane = lax.broadcasted_iota(jnp.int32, parts[0].shape, 1)
    low = lane < 64
    a, b, c, d = parts

    def halves(p, q):
        return (
            jnp.where(low, p, pltpu.roll(q, 64, 1)),
            jnp.where(low, pltpu.roll(p, 64, 1), q),
        )

    a, c = halves(a, c)
    b, d = halves(b, d)
    even = (lane // 32) % 2 == 0

    def quarters(p, q):
        return (
            jnp.where(even, p, pltpu.roll(q, 32, 1)),
            jnp.where(even, pltpu.roll(p, 96, 1), q),
        )

    a, b = quarters(a, b)
    c, d = quarters(c, d)
    return a, b, c, d


def range_kernel(raw, filt, matrices, twists, out, held):
    @pl.when(pl.program_id(0) == 0)
    def _():
        for part in range(2):
            rows = filt[pl.ds(part, 32, stride=2), :]
            tall = jnp.concatenate([rows, jnp.zeros((96, 128), F32)], axis=0).T
            total = tall[0:32]
            for m in range(1, 4):
                total = total + pltpu.roll(tall[32 * m : 32 * m + 32], 32 * m, 1)
            held[part] = total

    count = raw.shape[0]
    second, third = matrices[0:768, :], matrices[768:1536, :]
    last = jnp.concatenate([matrices[1536 + 256 * i : 1792 + 256 * i, :] for i in range(3)], axis=1)
    first = matrices[2304:2368, :][:, :192]
    tr = jnp.concatenate([twists[0]] * 2, axis=1)
    ti = jnp.concatenate([twists[1]] * 2, axis=1)
    res, ims = [], []
    for i in range(0, count, 2):
        x = jnp.concatenate([raw[i], raw[i + 1]], axis=1)
        y = dot(first, right_cols(x))
        zr, zi = times(y[:32], y[32:], tr, ti)
        res += [zr[:, :128], zr[:, 128:]]
        ims += [zi[:, :128], zi[:, 128:]]
    spectrum = dot(
        left_rows(jnp.concatenate(res, axis=0), jnp.concatenate(ims, axis=0)), second
    )
    sr = spectrum[:, :128].reshape(count, 32, 128)
    si = spectrum[:, 128:].reshape(count, 32, 128)
    sr, si = times(sr, si, held[0][None], held[1][None])
    back = dot(left_rows(sr.reshape(count * 32, 128), si.reshape(count * 32, 128)), third)
    br = back[:, :128].reshape(count, 32, 128)
    bi = back[:, 128:].reshape(count, 32, 128)
    br, bi = times(br, bi, twists[2][None], twists[3][None])
    done = []
    for c in range(0, 4, 2):
        cols = []
        for cc in (c, c + 1):
            rows = []
            for line in range(4):
                rows += [br[line * 4 + cc], bi[line * 4 + cc]]
            cols.append(jnp.concatenate(rows, axis=0))
        y = dot(last, right_cols(jnp.concatenate(cols, axis=1)))
        done += [y[:, :128], y[:, 128:]]
    for q, block in enumerate(swap_blocks(done)):
        for nt in range(32):
            out[int(PLACE[4 * nt + q])] = block[8 * nt : 8 * nt + 8]


def compress(raw_rows, filt_rows, start, groups):
    matrices, twists = range_tables()
    return pl.pallas_call(
        range_kernel,
        grid=(groups,),
        in_specs=[
            pl.BlockSpec((16, 64, 128), lambda g: (g + start, 0, 0)),
            pl.BlockSpec((64, 128), lambda g: (0, 0)),
            pl.BlockSpec(matrices.shape, lambda g: (0, 0)),
            pl.BlockSpec(twists.shape, lambda g: (0, 0, 0)),
        ],
        out_specs=pl.BlockSpec((128, 8, 128), lambda g: (0, g, 0)),
        out_shape=jax.ShapeDtypeStruct((128, 8 * groups, 128), F32),
        scratch_shapes=[pltpu.VMEM((2, 32, 128), F32)],
        compiler_params=pltpu.CompilerParams(vmem_limit_bytes=RANGE_VMEM),
        cost_estimate=pl.CostEstimate(
            flops=10**9 * groups, bytes_accessed=2**20 * groups, transcendentals=0
        ),
        name="range_compress",
    )(raw_rows, filt_rows, matrices, twists)


def transform_lines(turned, table, put):
    for jj in range(4):
        x = jnp.concatenate([turned[:, jj, :], turned[:, 4 + jj, :]], axis=0)
        f = table[jj]
        put(jj, dot(jnp.concatenate([f[:, :256], f], axis=1), right_cols(x)))


def line_kernel(turned, table, out):
    def put(jj, y):
        out[jj] = y

    transform_lines(turned, table, put)


def doppler_part(turned, start):
    table, _ = line_tables()
    groups = turned.shape[1] // 8
    return pl.pallas_call(
        line_kernel,
        grid=(groups,),
        in_specs=[
            pl.BlockSpec((128, 8, 128), lambda g: (0, g, 0)),
            pl.BlockSpec((4, 256, 512), lambda g: (g + start, 0, 0)),
        ],
        out_specs=pl.BlockSpec((4, 256, 128), lambda g: (g, 0, 0)),
        out_shape=jax.ShapeDtypeStruct((4 * groups, 256, 128), F32),
        compiler_params=pltpu.CompilerParams(vmem_limit_bytes=32 * 2**20),
        cost_estimate=pl.CostEstimate(
            flops=10**9 * groups, bytes_accessed=2**20 * groups, transcendentals=0
        ),
        name="doppler_part",
    )(turned, table)


def mix_kernel(count, ch, turned, table, eye, weights, *refs):
    earlier, (own, send, near, far, held) = refs[:count], refs[count:]
    group = pl.program_id(0)

    def put(jj, y):
        held[group * 4 + jj] = y

    transform_lines(turned, table, put)

    @pl.when(group == pl.num_programs(0) - 1)
    def _():
        first = ch[0] == 0

        def step(q, carry):
            rows = pl.ds(pl.multiple_of(q * 8, 8), 8)
            later = pl.ds(pl.multiple_of(128 + q * 8, 8), 8)
            lines = []
            for ref in (*earlier, held):
                lines += [(ref[j, rows, :], ref[j, later, :]) for j in range(ref.shape[0])]
            spectrum = small_fft(lines, -1)
            re = jnp.concatenate([v[0] for v in spectrum], axis=0)
            im = jnp.concatenate([v[1] for v in spectrum], axis=0)
            high, low = split(jnp.concatenate([re, im], axis=0))
            flat = lax.dot_general(
                eye[...],
                jnp.concatenate([high, low], axis=1),
                (((1,), (1,)), ((), ())),
                preferred_element_type=F32,
            )
            mr = mi = None
            for c in range(4):
                dr, di = flat[32 * c : 32 * c + 32, :128], flat[32 * c : 32 * c + 32, 128:]
                wr, wi = weights[0, c, pl.ds(q, 1), :], weights[1, c, pl.ds(q, 1), :]
                pr, pi = times(dr, di, wr, wi)
                mr, mi = (pr, pi) if mr is None else (mr + pr, mi + pi)
            for part, m in enumerate((mr, mi)):
                low24, high24 = m[:24], m[8:]
                own[q, part] = jnp.where(first, low24, high24)
                send[q, part] = jnp.where(first, high24, low24)
                near[q, part] = jnp.where(first, m[:8], m[24:])
                far[q, part] = jnp.where(first, m[24:], m[:8])
            return carry

        lax.fori_loop(0, 16, step, 0)


def doppler_mix(ch, turned, start, earlier, weights):
    table, eye = line_tables()
    groups = turned.shape[1] // 8
    wide = jax.ShapeDtypeStruct((16, 2, 24, 128), F32)
    thin = jax.ShapeDtypeStruct((16, 2, 8, 128), F32)
    whole = lambda n: (lambda g, *_: (0,) * n)
    return pl.pallas_call(
        functools.partial(mix_kernel, len(earlier)),
        grid_spec=pltpu.PrefetchScalarGridSpec(
            num_scalar_prefetch=1,
            grid=(groups,),
            in_specs=[
                pl.BlockSpec((128, 8, 128), lambda g, *_: (0, g, 0)),
                pl.BlockSpec((4, 256, 512), lambda g, *_: (g + start, 0, 0)),
                pl.BlockSpec((128, 256), whole(2)),
                pl.BlockSpec((2, 4, 16, 128), whole(4)),
                *[pl.BlockSpec(e.shape, whole(3)) for e in earlier],
            ],
            out_specs=[
                pl.BlockSpec(wide.shape, whole(4)),
                pl.BlockSpec(wide.shape, whole(4)),
                pl.BlockSpec(thin.shape, whole(4)),
                pl.BlockSpec(thin.shape, whole(4)),
            ],
            scratch_shapes=[pltpu.VMEM((4 * groups, 256, 128), F32)],
        ),
        out_shape=[wide, wide, thin, thin],
        compiler_params=pltpu.CompilerParams(vmem_limit_bytes=32 * 2**20),
        cost_estimate=pl.CostEstimate(
            flops=10**9 * groups, bytes_accessed=2**20 * groups, transcendentals=0
        ),
        name="doppler_mix",
    )(ch, turned, table, eye, weights, *earlier)


def focus_kernel(own, got, near, far, select, coef, az, right, twist, out, held):
    def step(q, carry):
        cols = []
        for part in range(2):
            cols.append(
                jnp.concatenate([own[q, part] + got[q, part], near[q, part] + far[q, part]], axis=0)
            )
        high, low = split(jnp.concatenate(cols, axis=1))
        taps = dot(select[...], jnp.concatenate([high, low], axis=0))
        moved = None
        for k in range(REACH):
            scale = coef[k, pl.ds(q, 1), :]
            term = taps[16 * k : 16 * k + 16] * jnp.concatenate([scale, scale], axis=1)
            moved = term if moved is None else moved + term
        fr, fi = times(moved[:, :128], moved[:, 128:], az[0, q], az[1, q])
        rows = pl.ds(pl.multiple_of(q * 16, 16), 16)
        held[0, rows, :] = fr
        held[1, rows, :] = fi
        return carry

    lax.fori_loop(0, 16, step, 0)
    y = dot(left_rows(held[0], held[1]), right[...])
    values = []
    for q in range(16):
        rows = y[16 * q : 16 * q + 16]
        values.append(times(rows[:, :128], rows[:, 128:], twist[0, q : q + 1], twist[1, q : q + 1]))
    for n, (re, im) in enumerate(small_fft(values, 1)):
        out[0, :, 128 * n : 128 * n + 128] = re
        out[1, :, 128 * n : 128 * n + 128] = im


def focus(own, got, near, far, select, coef, az):
    right, twist = focus_tables()
    return pl.pallas_call(
        focus_kernel,
        out_shape=jax.ShapeDtypeStruct((2, 16, 2048), F32),
        scratch_shapes=[pltpu.VMEM((2, 256, 128), F32)],
        compiler_params=pltpu.CompilerParams(vmem_limit_bytes=48 * 2**20),
        name="focus",
    )(own, got, near, far, select, coef, az, right, twist)


def tap_select(band_offset, band_width, ch):
    tap = jnp.arange(REACH, dtype=jnp.int32)[:, None, None]
    row = (jnp.arange(32, dtype=jnp.int32) + REACH * (1 - ch)) % 32
    target = jnp.arange(16, dtype=jnp.int32)[None, :, None] + REACH + band_offset[None, :, None] + tap
    hit = (row[None, None, :] == target) & (tap < band_width[None, :, None])
    hit = hit.astype(BF16).reshape(REACH * 16, 32)
    return jnp.concatenate([hit, hit], axis=1)


def body(raw, range_filter, recon, rcmc_coef, band_offset, band_width, az_filter):
    ch = lax.axis_index("ch")
    blocks = lax.axis_size(BLK)
    raw_rows = raw.reshape(16, 4, 2, 32, 128).transpose(0, 1, 3, 2, 4).reshape(64, 64, 128)
    filt_rows = range_filter.reshape(2, 32, 128).transpose(1, 0, 2).reshape(64, 128)
    starts = [sum(PARTS[:i]) for i in range(len(PARTS))]
    turned = []
    for i, (start, groups) in enumerate(zip(starts, PARTS)):
        pieces = compress(raw_rows, filt_rows, start, groups)
        if i == 0:
            (pieces, recon, rcmc_coef, az_filter, band_offset) = lax.optimization_barrier(
                (pieces, recon, rcmc_coef, az_filter, band_offset)
            )
        turned.append(lax.all_to_all(pieces, TURN, split_axis=0, concat_axis=0, tiled=True))
    weights = lax.dynamic_slice_in_dim(recon, ch * 4, 4, 1)
    weights = weights.reshape(2, 4, 128, 16).transpose(0, 1, 3, 2)
    coef = rcmc_coef.reshape(REACH, 128, 16).transpose(0, 2, 1)
    az = az_filter.reshape(2, 128, 16, 16).transpose(0, 2, 3, 1)
    select = tap_select(band_offset, band_width, ch)
    earlier = [doppler_part(t, start) for t, start in zip(turned[:-1], starts)]
    last, coef, az, select = lax.optimization_barrier((turned[-1], coef, az, select))
    own, send, near, far = doppler_mix(ch.reshape(1), last, starts[-1], earlier, weights)

    total = 2 * blocks
    cross = [(i, i + 1 if i % 2 else i - 1) for i in range(total)]
    along = [(i, i - 2 if i % 2 else i + 2) for i in range(total)]
    inside = lambda pairs: [(s, d) for s, d in pairs if 0 <= d < total]
    near = lax.ppermute(near, EVERY, inside(cross))
    far = lax.ppermute(far, EVERY, inside(along))
    got = lax.ppermute(send, "ch", [(0, 1), (1, 0)])
    image = focus(own, got, near, far, select, coef, az)
    return image.transpose(0, 2, 1)


def solution(mesh):
    grid = jax.sharding.Mesh(mesh.devices.reshape(4, 4, 8, 2), EVERY)
    return jax.shard_map(
        body,
        mesh=grid,
        in_specs=(
            P(BLK, "ch", None, None),
            P(),
            P(),
            P(),
            P(EVERY),
            P(EVERY),
            P(None, None, EVERY),
        ),
        out_specs=P(None, None, EVERY),
        check_vma=False,
    )
```

time: 367 us -> 105 us (0.29); the launches traced: 361 us -> 104 us
  local copies, waits for them, and re-layouts: 148 us -> 7.47 us
  matrix products: 60.1 us -> 0 us
  other arithmetic: 40.1 us -> 0.21 us
  Pallas kernels: 0 us -> 19.5 us
  waiting for transfers between devices: 72.8 us -> 55.3 us
  between operations: 14.1 us -> 0.18 us
  starting transfers between devices: 25.6 us -> 21.7 us
    dot_general x9 -> x0, matrix products: 59 us -> none  [complex_dot(): result = jnp.einsum(joined, stacked, blocks, precision=HIGHEST_MODE)]
    unnamed x16 -> x18, local copies, waits for them, and re-layouts: 50.9 us -> 2.23 us
    another operation x12 -> x0, local copies, waits for them, and re-layouts: 31.8 us -> none  [the longest x9 26.8 us: complex_dot(): stacked = jnp.stack([left_re, left_im], 0)]
    psum x1 -> x0, waiting for transfers between devices: 24.6 us -> none  [body(): total = lax.psum(partial_mix, 'ch')]
    unnamed x1 -> x0, other arithmetic: 21.3 us -> none
    all_to_all x2 -> x0, local copies, waits for them, and re-layouts: 21.1 us -> none  [body(): lax.all_to_all(compressed, 'blk', split_axis=3, concat_axis=0, tiled=True)]
    slice x5 -> x0, local copies, waits for them, and re-layouts: 19.7 us -> none  [the longest x1 9.46 us: body(): spectrum_re, spectrum_im = dft_last(raw[:, :, 0, :], raw[:, :, 1, :], -1.0)]
    pallas_call x0 -> x3, Pallas kernels: none -> 19.5 us  [the longest x1 9.4 us: compress(): pl.pallas_call(range_kernel, grid=(groups,), in_specs=[pl.BlockSpec((16,...]
  transfers between devices with their start and end apart: 4 -> 4, of which waited for: 3 -> 3; matrix products, arithmetic and copies ran while one was open for 2% -> 5% of each run, Pallas kernels for 0% -> 0%
where the time goes in v1:
time: 105 us; the launch traced here: 104 us
  waiting for transfers between devices  55.3 us (53%)
  starting transfers between devices  21.7 us (21%)
  Pallas kernels  19.5 us (19%)
  local copies, waits for them, and re-layouts  7.47 us (7%)
    all_to_all x1, waiting for transfers between devices, body(): lax.all_to_all(pieces, TURN, split_axis=0, concat_axis=0, tiled=True)  46.3 us
    all_to_all x1, starting transfers between devices, body(): lax.all_to_all(pieces, TURN, split_axis=0, concat_axis=0, tiled=True)  15.7 us
    pallas_call x1, Pallas kernels, compress(): pl.pallas_call(range_kernel, grid=(groups,), in_specs=[pl.BlockSpec((16,...  9.4 us
    pallas_call x1, Pallas kernels, doppler_mix(): pl.pallas_call(functools.partial(mix_kernel, len(earlier)), grid_spec=plt...  6.66 us
    ppermute x1, waiting for transfers between devices, body(): near = lax.ppermute(near, EVERY, inside(cross))  4.56 us
    ppermute x1, waiting for transfers between devices, body(): far = lax.ppermute(far, EVERY, inside(along))  4.43 us
    reshape x2, local copies, waits for them, and re-layouts, body(): az = az_filter.reshape(2, 128, 16, 16).transpose(0, 2, 3, 1)  4.25 us
    ppermute x1, starting transfers between devices, body(): near = lax.ppermute(near, EVERY, inside(cross))  3.84 us
  transfers between devices with their start and end apart: 4, of which 3 were waited for; matrix products, arithmetic and copies ran while one was open for 5% of the time, Pallas kernels for 0%

profile of v1, /device:TPU:2, one launch (start us, length us, event | category | flops | bytes accessed | tf_op | source)
XLA Modules:
  0.0 104.3 jit_solution(17269138502226780492)
XLA Ops:
  0.0 9.4 %range_compress.1 = f32[128,32,128]{2,1,0:T(8,128)} custom-call(f32[64,64,128]{2,1,0:T(8,128)} %bitcast.24, f32[64,128]{1,0:T(8,128)} %bitcast.25, bf16[2368,256]{1,0:T(8,128)(2,1)} %constant.39.clone.matrices, f32[4,32,128]{2,1,0:T(8,128)} %constant.40.clone.twists), custom_call_target="tpu_custom_call" | custom-call | flops 4000000000 | bytes 4194304 | tf_op jit(solution)/shard_map/range_compress/pallas_call | solution.py:220
  9.4 15.7 %all-to-all-start = ((f32[128,32,128]{2,1,0:T(8,128)}), f32[128,32,128]{2,1,0:T(8,128)S(1)}, u32[]{:S(2)}, u32[]{:S(2)}) async-start(f32[128,32,128]{2,1,0:T(8,128)} %range_compress.1), calls=%async_computation | async-start | bytes 4194304 | tf_op jit(solution)/shard_map/all_to_all | solution.py:419
  25.1 0.2 reshape.94
  25.3 0.2 copy.23
  25.5 0.0 copy-start.7
  25.5 2.0 %reshape.95 = f32[2,128,16,16]{2,1,3,0:T(8,128)} reshape(f32[2,2048,16]{1,2,0:T(8,128)S(1)} %copy-done.5) | data formatting | bytes 524288 | tf_op jit(solution)/shard_map/reshape | solution.py:423
  27.5 2.2 %copy.24 = f32[2,128,16,16]{1,3,2,0:T(8,128)S(1)} copy(f32[2,128,16,16]{2,1,3,0:T(8,128)} %reshape.95) | data formatting | bytes 524288 | tf_op jit(solution)/shard_map/reshape | solution.py:423
  29.8 0.1 add.63
  29.9 0.1 add.65
  30.0 0.1 lt.29
  30.1 0.2 reshape.96
  30.3 0.2 copy.26
  30.5 0.1 compare_and_fusion
  30.6 0.1 add_convert_fusion.select
  30.7 46.3 %all-to-all-done.turned = f32[128,32,128]{2,1,0:T(8,128)S(1)} async-done(((f32[128,32,128]{2,1,0:T(8,128)}), f32[128,32,128]{2,1,0:T(8,128)S(1)}, u32[]{:S(2)}, u32[]{:S(2)}) %all-to-all-start) | async-done | bytes 2097184 | tf_op jit(solution)/shard_map/all_to_all | solution.py:419
  77.0 2.2 %copy-done.3 = bf16[16,256,512]{2,1,0:T(8,128)(2,1)S(1)} copy-done((bf16[16,256,512]{2,1,0:T(8,128)(2,1)S(1)}, bf16[16,256,512]{2,1,0:T(8,128)(2,1)}, u32[]{:S(2)}) %copy-start.3) | copy-done | bytes 4194328
  79.2 6.7 %doppler_mix.1 = (f32[16,2,24,128]{3,2,1,0:T(8,128)S(1)}, f32[16,2,24,128]{3,2,1,0:T(8,128)S(1)}, f32[16,2,8,128]{3,2,1,0:T(8,128)S(1)}, f32[16,2,8,128]{3,2,1,0:T(8,128)S(1)}) custom-call(s32[1]{0:T(128)} %bitcast.ch, f32[128,32,128]{2,1,0:T(8,128)S(1)} %all-to-all-done.turned, bf16[16,256,512]{2,1,0:T(8,128)(2,1)S(1)} %copy-done.3, ...), custom_call_target="tpu_custom_call" | custom-call | flops 4000000000 | bytes 4194304 | tf_op jit(solution)/shard_map/doppler_mix/pallas_call | solution.py:326
  85.8 0.1 collective-permute-start
  85.9 3.8 %collective-permute-start.1 = (f32[16,2,8,128]{3,2,1,0:T(8,128)S(1)}, f32[16,2,8,128]{3,2,1,0:T(8,128)S(1)}, u32[]{:S(2)}, u32[]{:S(2)}) collective-permute-start(f32[16,2,8,128]{3,2,1,0:T(8,128)S(1)} %get-tuple-element.26), channel_id=1, source_target_pairs={{1,2},{2,1},{3,4},{4,3},{5,6},{6,5},{7,8},{8,7},{9,10},{10,9},{11,... | collective-permute-start | bytes 393224 | tf_op jit(solution)/shard_map/ppermute | solution.py:433
  89.8 2.1 %collective-permute-start.2 = (f32[16,2,8,128]{3,2,1,0:T(8,128)S(1)}, f32[16,2,8,128]{3,2,1,0:T(8,128)S(1)}, u32[]{:S(2)}, u32[]{:S(2)}) collective-permute-start(f32[16,2,8,128]{3,2,1,0:T(8,128)S(1)} %get-tuple-element.27), channel_id=1, source_target_pairs={{0,2},{2,4},{3,1},{4,6},{5,3},{6,8},{7,5},{8,10},{9,7},{10,12},{11... | collective-permute-start | bytes 393224 | tf_op jit(solution)/shard_map/ppermute | solution.py:434
  91.9 4.6 %collective-permute-done.1.near = f32[16,2,8,128]{3,2,1,0:T(8,128)S(1)} collective-permute-done((f32[16,2,8,128]{3,2,1,0:T(8,128)S(1)}, f32[16,2,8,128]{3,2,1,0:T(8,128)S(1)}, u32[]{:S(2)}, u32[]{:S(2)}) %collective-permute-start.1) | collective-permute-done | bytes 131104 | tf_op jit(solution)/shard_map/ppermute | solution.py:433
  96.4 4.4 %collective-permute-done.2.far = f32[16,2,8,128]{3,2,1,0:T(8,128)S(1)} collective-permute-done((f32[16,2,8,128]{3,2,1,0:T(8,128)S(1)}, f32[16,2,8,128]{3,2,1,0:T(8,128)S(1)}, u32[]{:S(2)}, u32[]{:S(2)}) %collective-permute-start.2) | collective-permute-done | bytes 131104 | tf_op jit(solution)/shard_map/ppermute | solution.py:434
  100.9 0.0 collective-permute-done.got
  100.9 3.4 %focus.1 = f32[2,16,2048]{2,1,0:T(8,128)} custom-call(f32[16,2,24,128]{3,2,1,0:T(8,128)S(1)} %get-tuple-element.24.own, f32[16,2,24,128]{3,2,1,0:T(8,128)S(1)} %collective-permute-done.got, f32[16,2,8,128]{3,2,1,0:T(8,128)S(1)} %collective-permute-done.1.near, f32[16,2,8,128]{3,2,1,0:T(8,128)S(1)} %collective-permute-done.2.far, ...), custom_call_target="tpu_custom_call" | custom-call | tf_op jit(solution)/shard_map/focus/pallas_call | solution.py:388
  (24 shorter events, 0.1 us)
Async XLA Ops:
  0.0 30.1 %copy-start = (f32[2,8,2048]{2,1,0:T(8,128)S(1)}, f32[2,8,2048]{2,1,0:T(8,128)}, u32[]{:S(2)}) copy-start(f32[2,8,2048]{2,1,0:T(8,128)} %param.15) | copy-start | bytes 393220
  9.4 15.7 %copy-start.6 = (f32[8,2048]{1,0:T(8,128)S(1)}, f32[8,2048]{1,0:T(8,128)}, u32[]{:S(2)}) copy-start(f32[8,2048]{1,0:T(8,128)} %param.16) | copy-start | bytes 196612
  9.4 16.1 %copy-start.5 = (f32[2,2048,16]{1,2,0:T(8,128)S(1)}, f32[2,2048,16]{1,2,0:T(8,128)}, u32[]{:S(2)}) copy-start(f32[2,2048,16]{1,2,0:T(8,128)} %param.19) | copy-start | bytes 786436
  9.4 67.6 %all-to-all-start = ((f32[128,32,128]{2,1,0:T(8,128)}), f32[128,32,128]{2,1,0:T(8,128)S(1)}, u32[]{:S(2)}, u32[]{:S(2)}) async-start(f32[128,32,128]{2,1,0:T(8,128)} %range_compress.1), calls=%async_computation | async-start | bytes 4194304 | tf_op jit(solution)/shard_map/all_to_all | solution.py:419
  25.5 4.3 %copy-start.8 = (s32[16]{0:T(128)S(1)}, s32[16]{0:T(128)}, u32[]{:S(2)}) copy-start(s32[16]{0:T(128)} %param.17) | copy-start | bytes 196
  25.5 4.5 %copy-start.7 = (s32[16]{0:T(128)S(1)}, s32[16]{0:T(128)}, u32[]{:S(2)}) copy-start(s32[16]{0:T(128)} %param.18) | copy-start | bytes 196
  27.5 49.4 %copy-start.4 = (bf16[128,256]{1,0:T(8,128)(2,1)S(1)}, bf16[128,256]{1,0:T(8,128)(2,1)}, u32[]{:S(2)}) copy-start(bf16[128,256]{1,0:T(8,128)(2,1)} %constant.42.clone.eye) | copy-start | bytes 196612
  77.0 2.2 %copy-start.3 = (bf16[16,256,512]{2,1,0:T(8,128)(2,1)S(1)}, bf16[16,256,512]{2,1,0:T(8,128)(2,1)}, u32[]{:S(2)}) copy-start(bf16[16,256,512]{2,1,0:T(8,128)(2,1)} %constant.41.clone.table) | copy-start | bytes 12582916
  79.2 21.7 %copy-start.1 = (bf16[768,256]{1,0:T(8,128)(2,1)S(1)}, bf16[768,256]{1,0:T(8,128)(2,1)}, u32[]{:S(2)}) copy-start(bf16[768,256]{1,0:T(8,128)(2,1)} %constant.43.clone.right) | copy-start | bytes 1179652
  79.2 21.7 %copy-start.2 = (f32[2,16,128]{2,1,0:T(8,128)S(1)}, f32[2,16,128]{2,1,0:T(8,128)}, u32[]{:S(2)}) copy-start(f32[2,16,128]{2,1,0:T(8,128)} %constant.44.clone.twist) | copy-start | bytes 49156
  85.8 15.0 %collective-permute-start = (f32[16,2,24,128]{3,2,1,0:T(8,128)S(1)}, f32[16,2,24,128]{3,2,1,0:T(8,128)S(1)}, u32[]{:S(2)}, u32[]{:S(2)}) collective-permute-start(f32[16,2,24,128]{3,2,1,0:T(8,128)S(1)} %get-tuple-element.25), channel_id=1, source_target_pairs={{0,1},{1,0},{2,3},{3,2},{4,5},{5,4},{6,7},{7,6},{8,9},{9,8},{10,11... | collective-permute-start | bytes 1179656 | tf_op jit(solution)/shard_map/ppermute | solution.py:435
  85.9 10.5 %collective-permute-start.1 = (f32[16,2,8,128]{3,2,1,0:T(8,128)S(1)}, f32[16,2,8,128]{3,2,1,0:T(8,128)S(1)}, u32[]{:S(2)}, u32[]{:S(2)}) collective-permute-start(f32[16,2,8,128]{3,2,1,0:T(8,128)S(1)} %get-tuple-element.26), channel_id=1, source_target_pairs={{1,2},{2,1},{3,4},{4,3},{5,6},{6,5},{7,8},{8,7},{9,10},{10,9},{11,... | collective-permute-start | bytes 393224 | tf_op jit(solution)/shard_map/ppermute | solution.py:433
  89.8 11.1 %collective-permute-start.2 = (f32[16,2,8,128]{3,2,1,0:T(8,128)S(1)}, f32[16,2,8,128]{3,2,1,0:T(8,128)S(1)}, u32[]{:S(2)}, u32[]{:S(2)}) collective-permute-start(f32[16,2,8,128]{3,2,1,0:T(8,128)S(1)} %get-tuple-element.27), channel_id=1, source_target_pairs={{0,2},{2,4},{3,1},{4,6},{5,3},{6,8},{7,5},{8,10},{9,7},{10,12},{11... | collective-permute-start | bytes 393224 | tf_op jit(solution)/shard_map/ppermute | solution.py:434

commit v2 on v1

v2 whole, which is shorter than its diff:
```python
import functools
import itertools
import math

import jax
import jax.numpy as jnp
import ml_dtypes
import numpy as np
from jax import lax
from jax.experimental import pallas as pl
from jax.experimental.pallas import tpu as pltpu
from jax.sharding import PartitionSpec as P

REACH = 8
BF16 = jnp.bfloat16
F32 = jnp.float32
RANGE_VMEM = 60 * 2**20
UNROLL = 16
CHIP = np.arange(128).reshape(4, 4, 8).transpose(0, 2, 1).reshape(128)
PLACE = np.argsort(CHIP)
TURN = ("ch", "x", "z", "y")
BLK = ("x", "y", "z")
EVERY = ("x", "y", "z", "ch")


def phase(rows, cols, length, sign):
    angle = sign * 2.0 * np.pi * ((np.outer(rows, cols) % length) / length)
    return np.cos(angle), np.sin(angle)


def pair(table):
    high = table.astype(np.float32).astype(ml_dtypes.bfloat16)
    low = (table - high.astype(np.float64)).astype(np.float32).astype(ml_dtypes.bfloat16)
    return high, low


def as_left(table):
    high, low = pair(table)
    return np.concatenate([high, high, low], axis=1)


def as_right(table):
    high, low = pair(table)
    return np.concatenate([high, high, low], axis=0)


def right_matrix(cosine, sine, scale=1.0):
    return np.block([[cosine, sine], [-sine, cosine]]) * scale


@functools.cache
def range_tables():
    t = np.arange(32)
    lane = np.arange(128)
    c32, s32 = phase(t, t, 32, -1)
    left = np.zeros((64, 32, 2))
    left[:32, :, 0], left[:32, :, 1] = c32, -s32
    left[32:, :, 0], left[32:, :, 1] = s32, c32
    first = as_left(left.reshape(64, 64))
    twist_in = np.stack(phase(t, lane, 4096, -1)).astype(np.float32)
    kl = 4 * (lane % 32) + lane // 32
    second = as_right(right_matrix(*phase(lane, kl, 128, -1)))
    third = as_right(right_matrix(*phase(kl, lane, 128, 1), scale=1.0 / 4096))
    twist_out = np.stack(phase(t, lane, 4096, 1)).astype(np.float32)
    c32, s32 = phase(t, t, 32, 1)
    high, low = pair(np.block([[c32, -s32], [s32, c32]]))
    last = np.block([[high, high], [low, np.zeros_like(low)]])
    last = np.pad(last, ((0, 0), (0, 128)))
    high, low = first[:, :64], first[:, 128:]
    first = np.block([[high, high], [low, np.zeros_like(low)]])
    first = np.pad(first, ((0, 0), (0, 128)))
    matrices = np.concatenate([second, third, last, first], axis=0)
    return matrices, np.concatenate([twist_in, twist_out], axis=0)


@functools.cache
def line_tables():
    row = np.arange(128)
    fb = 16 * (row % 8) + row // 8
    c, s = phase(fb, 16 * CHIP, 2048, -1)
    high, low = pair(np.block([[c, -s], [s, c]]))
    table = np.concatenate([high, low], axis=1)
    twist = np.stack(phase(fb, np.arange(16), 2048, -1)).astype(np.float32)
    eye = np.eye(128).astype(ml_dtypes.bfloat16)
    return table, twist, np.concatenate([eye, eye], axis=1)


@functools.cache
def focus_tables():
    lane = np.arange(128)
    right = as_right(right_matrix(*phase(lane, lane, 128, 1), scale=1.0 / 2048))
    twist = np.stack(phase(np.arange(16), lane, 2048, 1)).astype(np.float32)
    return right, twist


def split(x):
    high = x.astype(BF16)
    return high, (x - high.astype(F32)).astype(BF16)


def dot(left, right):
    return jnp.dot(left, right, preferred_element_type=F32)


def left_rows(re, im):
    rh, rl = split(re)
    ih, il = split(im)
    return jnp.concatenate([rh, ih, rl, il, rh, ih], axis=1)


def right_cols(x):
    high, low = split(x)
    return jnp.concatenate([high, low, high], axis=0)


def times(ar, ai, br, bi):
    return ar * br - ai * bi, ar * bi + ai * br


def small_fft(values, sign):
    count = len(values)
    if count == 1:
        return values
    even = small_fft(values[0::2], sign)
    odd = small_fft(values[1::2], sign)
    low, high = [], []
    for k in range(count // 2):
        (er, ei), (pr, pi) = even[k], odd[k]
        if k == 0:
            tr, ti = pr, pi
        elif 4 * k == count:
            tr, ti = (-pi, pr) if sign > 0 else (pi, -pr)
        else:
            c, s = math.cos(2 * math.pi * k / count), sign * math.sin(2 * math.pi * k / count)
            tr, ti = pr * c - pi * s, pr * s + pi * c
        low.append((er + tr, ei + ti))
        high.append((er - tr, ei - ti))
    return low + high


def swap_blocks(parts):
    lane = lax.broadcasted_iota(jnp.int32, parts[0].shape, 1)
    parts = list(parts)
    for step in (4, 2, 1):
        width = 16 * step
        low = (lane // width) % 2 == 0
        for i in range(8):
            if i & step:
                continue
            p, q = parts[i], parts[i + step]
            m = jnp.where(low, q, p)
            if step == 4:
                m = pltpu.roll(m, 64, 1)
            else:
                m = jnp.take_along_axis(m, lane ^ width, axis=1)
            parts[i] = jnp.where(low, p, m)
            parts[i + step] = jnp.where(low, m, q)
    return parts


def range_kernel(raw, filt, matrices, twists, out, raws, mats, small, reply, kept, held, ready, gone):
    loads = []
    for i, (source, target) in enumerate(
        [
            (matrices.at[1664:1792], mats.at[1664:1792]),
            (raw.at[0:16], raws.at[0:16]),
            (twists, small),
            (filt, reply),
            (matrices.at[0:768], mats.at[0:768]),
            (matrices.at[768:1536], mats.at[768:1536]),
            (matrices.at[1536:1664], mats.at[1536:1664]),
            (raw.at[16:32], raws.at[16:32]),
            (raw.at[32:48], raws.at[32:48]),
            (raw.at[48:64], raws.at[48:64]),
        ]
    ):
        copy = pltpu.make_async_copy(source, target, ready.at[i])
        copy.start()
        loads.append(copy)
    for i in range(4):
        loads[i].wait()
    first = mats[1664:1792, :][:, :128]
    tr = jnp.concatenate([small[0]] * 2, axis=1)
    ti = jnp.concatenate([small[1]] * 2, axis=1)
    turned_filter = []
    for part in range(2):
        rows = reply[pl.ds(part, 32, stride=2), :]
        tall = jnp.concatenate([rows, jnp.zeros((96, 128), F32)], axis=0).T
        total = tall[0:32]
        for m in range(1, 4):
            total = total + pltpu.roll(tall[32 * m : 32 * m + 32], 32 * m, 1)
        turned_filter.append(total)
    hr, hi = turned_filter
    stores = []
    for group in range(4):
        res, ims = [], []
        for i in range(16 * group, 16 * group + 16, 2):
            x = jnp.concatenate([raws[i], raws[i + 1]], axis=1)
            xh, xl = split(x)
            y = dot(first, jnp.concatenate([xh, xl], axis=0))
            y = y[:64] + y[64:]
            zr, zi = times(y[:32], y[32:], tr, ti)
            res += [zr[:, :128], zr[:, 128:]]
            ims += [zi[:, :128], zi[:, 128:]]
        if group == 0:
            for i in range(4, 10):
                loads[i].wait()
        second, third = mats[0:768, :], mats[768:1536, :]
        last = mats[1536:1664, :][:, :128]
        spectrum = dot(
            left_rows(jnp.concatenate(res, axis=0), jnp.concatenate(ims, axis=0)), second
        )
        sr = spectrum[:, :128].reshape(16, 32, 128)
        si = spectrum[:, 128:].reshape(16, 32, 128)
        sr, si = times(sr, si, hr[None], hi[None])
        back = dot(left_rows(sr.reshape(512, 128), si.reshape(512, 128)), third)
        br = back[:, :128].reshape(16, 32, 128)
        bi = back[:, 128:].reshape(16, 32, 128)
        br, bi = times(br, bi, small[2][None], small[3][None])
        for i in range(0, 16, 2):
            cols = [jnp.concatenate([br[k], bi[k]], axis=0) for k in (i, i + 1)]
            xh, xl = split(jnp.concatenate(cols, axis=1))
            y = dot(last, jnp.concatenate([xh, xl], axis=0))
            y = y[:64] + y[64:]
            for k in range(2):
                line, c = (i + k) // 4, (i + k) % 4
                for part in range(2):
                    kept[group % 2, c, pl.ds(part * 4 + line, 32, stride=8), :] = y[
                        32 * part : 32 * part + 32, 128 * k : 128 * k + 128
                    ]
        if group % 2 == 0:
            continue
        half = group // 2
        parts = [kept.at[g, c] for g in range(2) for c in range(4)]
        for i in range(32):
            blocks = swap_blocks([p[8 * i : 8 * i + 8, :] for p in parts])
            for d, block in enumerate(blocks):
                place = int(PLACE[4 * i + d // 2]) + 128 * (d % 2)
                held[half, place] = block
            if i % 8 == 7:
                for core in range(2):
                    spot = 128 * core + 4 * (i - 7)
                    copy = pltpu.make_async_copy(
                        held.at[half, spot : spot + 32],
                        out.at[spot : spot + 32, 8 * half : 8 * half + 8, :],
                        gone.at[len(stores)],
                    )
                    copy.start()
                    stores.append(copy)
    for copy in stores:
        copy.wait()


def compress(raw_rows, filt_rows):
    matrices, twists = range_tables()
    anywhere = pl.BlockSpec(memory_space=pl.ANY)
    return pl.pallas_call(
        range_kernel,
        in_specs=[anywhere] * 4,
        out_specs=anywhere,
        out_shape=jax.ShapeDtypeStruct((256, 16, 128), F32),
        scratch_shapes=[
            pltpu.VMEM((64, 64, 128), F32),
            pltpu.VMEM(matrices.shape, BF16),
            pltpu.VMEM((4, 32, 128), F32),
            pltpu.VMEM((64, 128), F32),
            pltpu.VMEM((2, 4, 256, 128), F32),
            pltpu.VMEM((2, 256, 8, 128), F32),
            pltpu.SemaphoreType.DMA((10,)),
            pltpu.SemaphoreType.DMA((16,)),
        ],
        compiler_params=pltpu.CompilerParams(vmem_limit_bytes=RANGE_VMEM),
        cost_estimate=pl.CostEstimate(flops=4 * 10**9, bytes_accessed=2**22, transcendentals=0),
        name="range_compress",
    )(raw_rows, filt_rows, matrices, twists)


def mix_kernel(ch, turned, table, twist, eye, weights, own, near, far, held):
    low = lax.broadcasted_iota(jnp.int32, (128, 128), 1) < 64
    f = table[...]
    f = jnp.concatenate([f[:, :256], f], axis=1)
    for half, line in itertools.product(range(2), range(4)):
        cols = [
            jnp.concatenate(
                [turned[128 * s : 128 * s + 128, half * 8 + part * 4 + line, :] for s in range(2)], 1
            )
            for part in range(2)
        ]
        y = dot(f, right_cols(jnp.concatenate(cols, axis=0)))
        pairs = []
        for part in range(2):
            a, b = y[128 * part : 128 * part + 128, :128], y[128 * part : 128 * part + 128, 128:]
            m = pltpu.roll(jnp.where(low, b, a), 64, 1)
            pairs.append((jnp.where(low, a, m), jnp.where(low, m, b)))
        for k in range(2):
            j = half * 8 + 4 * k + line
            re, im = pairs[0][k], pairs[1][k]
            if j:
                re, im = times(re, im, twist[0, :, j : j + 1], twist[1, :, j : j + 1])
            held[j, 0] = re
            held[j, 1] = im

    low_core = ch[0] == 0

    def step(q, carry):
        rows = pl.ds(pl.multiple_of(q * 8, 8), 8)
        lines = [(held[j, 0, rows, :], held[j, 1, rows, :]) for j in range(16)]
        spectrum = small_fft(lines, -1)
        re = jnp.concatenate([v[0] for v in spectrum], axis=0)
        im = jnp.concatenate([v[1] for v in spectrum], axis=0)
        high, rest = split(jnp.concatenate([re, im], axis=0))
        flat = lax.dot_general(
            eye[...],
            jnp.concatenate([high, rest], axis=1),
            (((1,), (1,)), ((), ())),
            preferred_element_type=F32,
        )
        mr = mi = None
        for c in range(8):
            dr, di = flat[16 * c : 16 * c + 16, :128], flat[16 * c : 16 * c + 16, 128:]
            wr, wi = weights[0, c, pl.ds(q, 1), :], weights[1, c, pl.ds(q, 1), :]
            pr, pi = times(dr, di, wr, wi)
            mr, mi = (pr, pi) if mr is None else (mr + pr, mi + pi)
        for part, m in enumerate((mr, mi)):
            own[q, part] = m
            near[q, part] = jnp.where(low_core, m[8:], m[:8])
            far[q, part] = jnp.where(low_core, m[:8], m[8:])
        return carry

    lax.fori_loop(0, 16, step, 0, unroll=UNROLL)


def doppler_mix(ch, turned, weights):
    table, twist, eye = line_tables()
    wide = jax.ShapeDtypeStruct((16, 2, 16, 128), F32)
    thin = jax.ShapeDtypeStruct((16, 2, 8, 128), F32)
    inside = pl.BlockSpec(memory_space=pltpu.VMEM)
    return pl.pallas_call(
        mix_kernel,
        in_specs=[pl.BlockSpec(memory_space=pltpu.SMEM)] + [inside] * 5,
        out_specs=[inside] * 3,
        out_shape=[wide, thin, thin],
        scratch_shapes=[pltpu.VMEM((16, 2, 128, 128), F32)],
        compiler_params=pltpu.CompilerParams(vmem_limit_bytes=24 * 2**20),
        cost_estimate=pl.CostEstimate(flops=4 * 10**9, bytes_accessed=2**22, transcendentals=0),
        name="doppler_mix",
    )(ch, turned, table, twist, eye, weights)


def focus_kernel(own, near, far, select, coef, az, right, twist, out, held):
    def step(q, carry):
        cols = []
        for part in range(2):
            cols.append(jnp.concatenate([own[q, part], near[q, part], far[q, part]], axis=0))
        high, low = split(jnp.concatenate(cols, axis=1))
        taps = dot(select[...], jnp.concatenate([high, low], axis=0))
        moved = None
        for k in range(REACH):
            scale = coef[k, pl.ds(q, 1), :]
            term = taps[16 * k : 16 * k + 16] * jnp.concatenate([scale, scale], axis=1)
            moved = term if moved is None else moved + term
        fr, fi = times(moved[:, :128], moved[:, 128:], az[0, q], az[1, q])
        rows = pl.ds(pl.multiple_of(q * 16, 16), 16)
        held[0, rows, :] = fr
        held[1, rows, :] = fi
        return carry

    lax.fori_loop(0, 16, step, 0, unroll=UNROLL)
    y = dot(left_rows(held[0], held[1]), right[...])
    values = []
    for q in range(16):
        rows = y[16 * q : 16 * q + 16]
        values.append(times(rows[:, :128], rows[:, 128:], twist[0, q : q + 1], twist[1, q : q + 1]))
    for n, (re, im) in enumerate(small_fft(values, 1)):
        out[0, :, 128 * n : 128 * n + 128] = re
        out[1, :, 128 * n : 128 * n + 128] = im


def focus(own, near, far, select, coef, az):
    right, twist = focus_tables()
    return pl.pallas_call(
        focus_kernel,
        out_shape=jax.ShapeDtypeStruct((2, 16, 2048), F32),
        scratch_shapes=[pltpu.VMEM((2, 256, 128), F32)],
        compiler_params=pltpu.CompilerParams(vmem_limit_bytes=48 * 2**20),
        name="focus",
    )(own, near, far, select, coef, az, right, twist)


def tap_select(band_offset, band_width, ch):
    tap = jnp.arange(REACH, dtype=jnp.int32)[:, None, None]
    eight = jnp.arange(8, dtype=jnp.int32)
    left, right = eight, eight + 24
    row = jnp.concatenate(
        [
            eight + 8,
            eight + 16,
            jnp.where(ch == 0, right, left),
            jnp.where(ch == 0, left, right),
        ]
    )
    target = jnp.arange(16, dtype=jnp.int32)[None, :, None] + REACH + band_offset[None, :, None] + tap
    hit = (row[None, None, :] == target) & (tap < band_width[None, :, None])
    hit = hit.astype(BF16).reshape(REACH * 16, 32)
    return jnp.concatenate([hit, hit], axis=1)


def body(raw, range_filter, recon, rcmc_coef, band_offset, band_width, az_filter):
    ch = lax.axis_index("ch")
    blocks = lax.axis_size(BLK)
    raw_rows = raw.reshape(16, 4, 2, 32, 128).transpose(0, 1, 3, 2, 4).reshape(64, 64, 128)
    filt_rows = range_filter.reshape(2, 32, 128).transpose(1, 0, 2).reshape(64, 128)
    pieces = compress(raw_rows, filt_rows)
    (pieces, recon, rcmc_coef, az_filter, band_offset) = lax.optimization_barrier(
        (pieces, recon, rcmc_coef, az_filter, band_offset)
    )
    turned = lax.all_to_all(pieces, TURN, split_axis=0, concat_axis=0, tiled=True)
    weights = recon.reshape(2, 8, 128, 16).transpose(0, 1, 3, 2)
    coef = rcmc_coef.reshape(REACH, 128, 16).transpose(0, 2, 1)
    az = az_filter.reshape(2, 128, 16, 16).transpose(0, 2, 3, 1)
    select = tap_select(band_offset, band_width, ch)
    turned, weights, coef, az, select = lax.optimization_barrier(
        (turned, weights, coef, az, select)
    )
    own, near, far = doppler_mix(ch.reshape(1), turned, weights)

    total = 2 * blocks
    cross = [(i, i + 1 if i % 2 else i - 1) for i in range(total)]
    cross = [(s, d) for s, d in cross if 0 <= d < total]
    far = lax.ppermute(far, EVERY, cross)
    near = lax.ppermute(near, "ch", [(0, 1), (1, 0)])
    image = focus(own, near, far, select, coef, az)
    return image.transpose(0, 2, 1)


def solution(mesh):
    grid = jax.sharding.Mesh(mesh.devices.reshape(4, 4, 8, 2), EVERY)
    return jax.shard_map(
        body,
        mesh=grid,
        in_specs=(
            P(BLK, "ch", None, None),
            P(),
            P(),
            P(),
            P(EVERY),
            P(EVERY),
            P(None, None, EVERY),
        ),
        out_specs=P(None, None, EVERY),
        check_vma=False,
    )
```

time: 105 us -> 91.1 us (0.87)
  Pallas kernels: 19.5 us -> 12.8 us
  waiting for transfers between devices: 55.3 us -> 50.3 us
  starting transfers between devices: 21.7 us -> 19.5 us
    pallas_call x2, Pallas kernels: 16.1 us -> 11.4 us  [the longest x1 7.99 us: compress(): pl.pallas_call(range_kernel, in_specs=[anywhere] * 4, out_specs=anywhere,...]
    ppermute x3 -> x2, waiting for transfers between devices: 8.99 us -> 5.74 us  [the longest x1 5.73 us: body(): far = lax.ppermute(far, EVERY, cross)]
    reshape x2, local copies, waits for them, and re-layouts: 0.37 us -> 2.86 us  [body(): weights = recon.reshape(2, 8, 128, 16).transpose(0, 1, 3, 2)]
    unnamed x18 -> x20, local copies, waits for them, and re-layouts: 2.23 us -> 0.07 us
    pallas_call x1, Pallas kernels: 3.44 us -> 1.4 us  [focus(): pl.pallas_call(focus_kernel, out_shape=jax.ShapeDtypeStruct((2, 16, 2048)...]
    all_to_all x1, waiting for transfers between devices: 46.3 us -> 44.5 us  [body(): lax.all_to_all(pieces, TURN, split_axis=0, concat_axis=0, tiled=True)]
    ppermute x3 -> x2, starting transfers between devices: 6.02 us -> 4.85 us  [the longest x1 4.75 us: body(): far = lax.ppermute(far, EVERY, cross)]
  transfers between devices with their start and end apart: 4 -> 3, of which waited for: 3 -> 2; matrix products, arithmetic and copies ran while one was open for 5% -> 9% of each run, Pallas kernels for 0% -> 0%
where the time goes in v2:
time: 91.1 us; the launch traced here: 90.9 us
  waiting for transfers between devices  50.3 us (55%)
  starting transfers between devices  19.5 us (21%)
  Pallas kernels  12.8 us (14%)
  local copies, waits for them, and re-layouts  7.77 us (9%)
    all_to_all x1, waiting for transfers between devices, body(): lax.all_to_all(pieces, TURN, split_axis=0, concat_axis=0, tiled=True)  44.5 us
    all_to_all x1, starting transfers between devices, body(): lax.all_to_all(pieces, TURN, split_axis=0, concat_axis=0, tiled=True)  14.7 us
    pallas_call x1, Pallas kernels, compress(): pl.pallas_call(range_kernel, in_specs=[anywhere] * 4, out_specs=anywhere,...  7.99 us
    ppermute x1, waiting for transfers between devices, body(): far = lax.ppermute(far, EVERY, cross)  5.73 us
    ppermute x1, starting transfers between devices, body(): far = lax.ppermute(far, EVERY, cross)  4.75 us
    reshape x2, local copies, waits for them, and re-layouts, body(): az = az_filter.reshape(2, 128, 16, 16).transpose(0, 2, 3, 1)  4.23 us
    pallas_call x1, Pallas kernels, doppler_mix(): pl.pallas_call(mix_kernel, in_specs=[pl.BlockSpec(memory_space=pltpu.SMEM...  3.38 us
    reshape x2, local copies, waits for them, and re-layouts, body(): weights = recon.reshape(2, 8, 128, 16).transpose(0, 1, 3, 2)  2.86 us
  transfers between devices with their start and end apart: 3, of which 2 were waited for; matrix products, arithmetic and copies ran while one was open for 9% of the time, Pallas kernels for 0%

profile of v2, /device:TPU:2, one launch (start us, length us, event | category | flops | bytes accessed | tf_op | source)
XLA Modules:
  0.0 90.9 jit_solution(2152639020095081027)
XLA Ops:
  0.0 8.0 %range_compress.1 = f32[256,16,128]{2,1,0:T(8,128)} custom-call(f32[64,64,128]{2,1,0:T(8,128)} %bitcast.24, f32[64,128]{1,0:T(8,128)} %bitcast.25, bf16[1792,256]{1,0:T(8,128)(2,1)} %constant.11.clone.matrices, f32[4,32,128]{2,1,0:T(8,128)} %constant.28.clone.twists), custom_call_target="tpu_custom_call" | custom-call | flops 4000000000 | bytes 4194304 | tf_op jit(solution)/shard_map/range_compress/pallas_call | solution.py:257
  8.0 14.7 %all-to-all-start = ((f32[256,16,128]{2,1,0:T(8,128)}), f32[256,16,128]{2,1,0:T(8,128)S(1)}, u32[]{:S(2)}, u32[]{:S(2)}) async-start(f32[256,16,128]{2,1,0:T(8,128)} %range_compress.1), calls=%async_computation | async-start | bytes 4194304 | tf_op jit(solution)/shard_map/all_to_all | solution.py:417
  22.7 1.3 %reshape.80 = f32[2,8,128,16]{3,2,1,0:T(8,128)} reshape(f32[2,8,2048]{2,1,0:T(8,128)S(1)} %copy-done.6) | data formatting | bytes 262144 | tf_op jit(solution)/shard_map/reshape | solution.py:418
  24.1 1.5 %copy.24 = f32[2,8,128,16]{2,3,1,0:T(8,128)S(1)} copy(f32[2,8,128,16]{3,2,1,0:T(8,128)} %reshape.80) | data formatting | bytes 262144 | tf_op jit(solution)/shard_map/reshape | solution.py:418
  25.6 0.2 reshape.81
  25.8 0.2 copy.25
  26.0 0.0 copy-start.8
  26.0 0.0 copy-start.2
  26.0 0.0 copy-start.3
  26.0 0.0 copy-start.4
  26.0 2.1 %reshape.82 = f32[2,128,16,16]{2,1,3,0:T(8,128)} reshape(f32[2,2048,16]{1,2,0:T(8,128)S(1)} %copy-done.5) | data formatting | bytes 524288 | tf_op jit(solution)/shard_map/reshape | solution.py:420
  28.1 2.2 %copy.26 = f32[2,128,16,16]{1,3,2,0:T(8,128)S(1)} copy(f32[2,128,16,16]{2,1,3,0:T(8,128)} %reshape.82) | data formatting | bytes 524288 | tf_op jit(solution)/shard_map/reshape | solution.py:420
  30.3 0.1 add.51
  30.4 0.1 add.53
  30.5 0.1 lt.19
  30.6 0.1 pad_add_fusion
  30.7 0.1 compare_and_fusion
  30.8 0.1 add_convert_fusion.select
  30.9 44.5 %all-to-all-done.turned = f32[256,16,128]{2,1,0:T(8,128)S(1)} async-done(((f32[256,16,128]{2,1,0:T(8,128)}), f32[256,16,128]{2,1,0:T(8,128)S(1)}, u32[]{:S(2)}, u32[]{:S(2)}) %all-to-all-start) | async-done | bytes 2097184 | tf_op jit(solution)/shard_map/all_to_all | solution.py:417
  75.5 3.4 %doppler_mix.1 = (f32[16,2,16,128]{3,2,1,0:T(8,128)S(1)}, f32[16,2,8,128]{3,2,1,0:T(8,128)S(1)}, f32[16,2,8,128]{3,2,1,0:T(8,128)S(1)}) custom-call(s32[1]{0:T(128)} %bitcast.ch, f32[256,16,128]{2,1,0:T(8,128)S(1)} %all-to-all-done.turned, bf16[256,512]{1,0:T(8,128)(2,1)S(1)} %copy-done.2, f32[2,128,16]{2,1,0:T(8,128)S(1)} %copy-done.3, ...), custom_call_target="tpu_custom_call" | custom-call | flops 4000000000 | bytes 4194304 | tf_op jit(solution)/shard_map/doppler_mix/pallas_call | solution.py:338
  78.9 0.1 collective-permute-start
  79.0 4.8 %collective-permute-start.1 = (f32[16,2,8,128]{3,2,1,0:T(8,128)S(1)}, f32[16,2,8,128]{3,2,1,0:T(8,128)S(1)}, u32[]{:S(2)}, u32[]{:S(2)}) collective-permute-start(f32[16,2,8,128]{3,2,1,0:T(8,128)S(1)} %get-tuple-element.27), channel_id=1, source_target_pairs={{1,2},{2,1},{3,4},{4,3},{5,6},{6,5},{7,8},{8,7},{9,10},{10,9},{11,... | collective-permute-start | bytes 393224 | tf_op jit(solution)/shard_map/ppermute | solution.py:430
  83.7 5.7 %collective-permute-done.1.far = f32[16,2,8,128]{3,2,1,0:T(8,128)S(1)} collective-permute-done((f32[16,2,8,128]{3,2,1,0:T(8,128)S(1)}, f32[16,2,8,128]{3,2,1,0:T(8,128)S(1)}, u32[]{:S(2)}, u32[]{:S(2)}) %collective-permute-start.1) | collective-permute-done | bytes 131104 | tf_op jit(solution)/shard_map/ppermute | solution.py:430
  89.5 1.4 %focus.1 = f32[2,16,2048]{2,1,0:T(8,128)} custom-call(f32[16,2,16,128]{3,2,1,0:T(8,128)S(1)} %get-tuple-element.25.own, f32[16,2,8,128]{3,2,1,0:T(8,128)S(1)} %collective-permute-done.near, f32[16,2,8,128]{3,2,1,0:T(8,128)S(1)} %collective-permute-done.1.far, bf16[128,64]{1,0:T(8,128)(2,1)S(1)} %add_convert_fusion.select, f32[8,16,128]{2,1,0:T(8,128)S(1)} %bitcast.22, ...), custom_call_target="tpu_custom_call" | custom-call | tf_op jit(solution)/shard_map/focus/pallas_call | solution.py:381
  (25 shorter events, 0.1 us)
Async XLA Ops:
  8.0 14.7 %copy-start.6 = (f32[2,8,2048]{2,1,0:T(8,128)S(1)}, f32[2,8,2048]{2,1,0:T(8,128)}, u32[]{:S(2)}) copy-start(f32[2,8,2048]{2,1,0:T(8,128)} %param.16) | copy-start | bytes 393220
  8.0 67.4 %all-to-all-start = ((f32[256,16,128]{2,1,0:T(8,128)}), f32[256,16,128]{2,1,0:T(8,128)S(1)}, u32[]{:S(2)}, u32[]{:S(2)}) async-start(f32[256,16,128]{2,1,0:T(8,128)} %range_compress.1), calls=%async_computation | async-start | bytes 4194304 | tf_op jit(solution)/shard_map/all_to_all | solution.py:417
  22.7 2.9 %copy-start.7 = (f32[8,2048]{1,0:T(8,128)S(1)}, f32[8,2048]{1,0:T(8,128)}, u32[]{:S(2)}) copy-start(f32[8,2048]{1,0:T(8,128)} %param.17) | copy-start | bytes 196612
  22.7 3.3 %copy-start.5 = (f32[2,2048,16]{1,2,0:T(8,128)S(1)}, f32[2,2048,16]{1,2,0:T(8,128)}, u32[]{:S(2)}) copy-start(f32[2,2048,16]{1,2,0:T(8,128)} %param.20) | copy-start | bytes 786436
  26.0 4.3 %copy-start.9 = (s32[16]{0:T(128)S(1)}, s32[16]{0:T(128)}, u32[]{:S(2)}) copy-start(s32[16]{0:T(128)} %param.18) | copy-start | bytes 196
  26.0 4.5 %copy-start.8 = (s32[16]{0:T(128)S(1)}, s32[16]{0:T(128)}, u32[]{:S(2)}) copy-start(s32[16]{0:T(128)} %param.19) | copy-start | bytes 196
  26.0 49.4 %copy-start.2 = (bf16[256,512]{1,0:T(8,128)(2,1)S(1)}, bf16[256,512]{1,0:T(8,128)(2,1)}, u32[]{:S(2)}) copy-start(bf16[256,512]{1,0:T(8,128)(2,1)} %constant.29.clone.table) | copy-start | bytes 786436
  26.0 49.4 %copy-start.3 = (f32[2,128,16]{2,1,0:T(8,128)S(1)}, f32[2,128,16]{2,1,0:T(8,128)}, u32[]{:S(2)}) copy-start(f32[2,128,16]{2,1,0:T(8,128)} %constant.30.clone.twist) | copy-start | bytes 49156
  26.0 49.4 %copy-start.4 = (bf16[128,256]{1,0:T(8,128)(2,1)S(1)}, bf16[128,256]{1,0:T(8,128)(2,1)}, u32[]{:S(2)}) copy-start(bf16[128,256]{1,0:T(8,128)(2,1)} %constant.31.clone.eye) | copy-start | bytes 196612
  75.4 14.0 %copy-start = (bf16[768,256]{1,0:T(8,128)(2,1)S(1)}, bf16[768,256]{1,0:T(8,128)(2,1)}, u32[]{:S(2)}) copy-start(bf16[768,256]{1,0:T(8,128)(2,1)} %constant.32.clone.right) | copy-start | bytes 1179652
  75.5 14.0 %copy-start.1 = (f32[2,16,128]{2,1,0:T(8,128)S(1)}, f32[2,16,128]{2,1,0:T(8,128)}, u32[]{:S(2)}) copy-start(f32[2,16,128]{2,1,0:T(8,128)} %constant.33.clone.twist) | copy-start | bytes 49156
  78.9 4.9 %collective-permute-start = (f32[16,2,8,128]{3,2,1,0:T(8,128)S(1)}, f32[16,2,8,128]{3,2,1,0:T(8,128)S(1)}, u32[]{:S(2)}, u32[]{:S(2)}) collective-permute-start(f32[16,2,8,128]{3,2,1,0:T(8,128)S(1)} %get-tuple-element.26), channel_id=1, source_target_pairs={{0,1},{1,0},{2,3},{3,2},{4,5},{5,4},{6,7},{7,6},{8,9},{9,8},{10,11... | collective-permute-start | bytes 393224 | tf_op jit(solution)/shard_map/ppermute | solution.py:431
  79.0 10.5 %collective-permute-start.1 = (f32[16,2,8,128]{3,2,1,0:T(8,128)S(1)}, f32[16,2,8,128]{3,2,1,0:T(8,128)S(1)}, u32[]{:S(2)}, u32[]{:S(2)}) collective-permute-start(f32[16,2,8,128]{3,2,1,0:T(8,128)S(1)} %get-tuple-element.27), channel_id=1, source_target_pairs={{1,2},{2,1},{3,4},{4,3},{5,6},{6,5},{7,8},{8,7},{9,10},{10,9},{11,... | collective-permute-start | bytes 393224 | tf_op jit(solution)/shard_map/ppermute | solution.py:430

commit v3 on v2

--- a/solution.py
+++ b/solution.py
@@ -1,5 +1,4 @@
 import functools
-import itertools
 import math
 
 import jax
@@ -16,6 +15,7 @@
 F32 = jnp.float32
 RANGE_VMEM = 60 * 2**20
 UNROLL = 16
+PITCH = 264
 CHIP = np.arange(128).reshape(4, 4, 8).transpose(0, 2, 1).reshape(128)
 PLACE = np.argsort(CHIP)
 TURN = ("ch", "x", "z", "y")
@@ -52,24 +52,12 @@
 def range_tables():
     t = np.arange(32)
     lane = np.arange(128)
-    c32, s32 = phase(t, t, 32, -1)
-    left = np.zeros((64, 32, 2))
-    left[:32, :, 0], left[:32, :, 1] = c32, -s32
-    left[32:, :, 0], left[32:, :, 1] = s32, c32
-    first = as_left(left.reshape(64, 64))
     twist_in = np.stack(phase(t, lane, 4096, -1)).astype(np.float32)
     kl = 4 * (lane % 32) + lane // 32
     second = as_right(right_matrix(*phase(lane, kl, 128, -1)))
     third = as_right(right_matrix(*phase(kl, lane, 128, 1), scale=1.0 / 4096))
     twist_out = np.stack(phase(t, lane, 4096, 1)).astype(np.float32)
-    c32, s32 = phase(t, t, 32, 1)
-    high, low = pair(np.block([[c32, -s32], [s32, c32]]))
-    last = np.block([[high, high], [low, np.zeros_like(low)]])
-    last = np.pad(last, ((0, 0), (0, 128)))
-    high, low = first[:, :64], first[:, 128:]
-    first = np.block([[high, high], [low, np.zeros_like(low)]])
-    first = np.pad(first, ((0, 0), (0, 128)))
-    matrices = np.concatenate([second, third, last, first], axis=0)
+    matrices = np.concatenate([second, third], axis=0)
     return matrices, np.concatenate([twist_in, twist_out], axis=0)
 
 
@@ -158,82 +146,73 @@
     return parts
 
 
+def over_rows(table, row):
+    return jnp.broadcast_to(table[row : row + 1, :], (8, 128))
+
+
 def range_kernel(raw, filt, matrices, twists, out, raws, mats, small, reply, kept, held, ready, gone):
+    def line_copy(i):
+        return raw.at[256 * i : 256 * i + 256], raws.at[PITCH * i : PITCH * i + 256]
+
     loads = []
     for i, (source, target) in enumerate(
         [
-            (matrices.at[1664:1792], mats.at[1664:1792]),
-            (raw.at[0:16], raws.at[0:16]),
+            *[line_copy(i) for i in range(8)],
             (twists, small),
             (filt, reply),
-            (matrices.at[0:768], mats.at[0:768]),
-            (matrices.at[768:1536], mats.at[768:1536]),
-            (matrices.at[1536:1664], mats.at[1536:1664]),
-            (raw.at[16:32], raws.at[16:32]),
-            (raw.at[32:48], raws.at[32:48]),
-            (raw.at[48:64], raws.at[48:64]),
+            (matrices, mats),
+            *[line_copy(i) for i in range(8, 16)],
         ]
     ):
         copy = pltpu.make_async_copy(source, target, ready.at[i])
         copy.start()
         loads.append(copy)
-    for i in range(4):
-        loads[i].wait()
-    first = mats[1664:1792, :][:, :128]
-    tr = jnp.concatenate([small[0]] * 2, axis=1)
-    ti = jnp.concatenate([small[1]] * 2, axis=1)
-    turned_filter = []
+    for copy in loads[:10]:
+        copy.wait()
+    spectrum_filter = []
     for part in range(2):
         rows = reply[pl.ds(part, 32, stride=2), :]
         tall = jnp.concatenate([rows, jnp.zeros((96, 128), F32)], axis=0).T
         total = tall[0:32]
         for m in range(1, 4):
             total = total + pltpu.roll(tall[32 * m : 32 * m + 32], 32 * m, 1)
-        turned_filter.append(total)
-    hr, hi = turned_filter
+        spectrum_filter.append(total)
+    hr, hi = spectrum_filter
+
+    def apply(values, re, im):
+        return [
+            times(vr, vi, over_rows(re, k), over_rows(im, k)) for k, (vr, vi) in enumerate(values)
+        ]
+
+    def lanes(values, matrix):
+        y = dot(
+            left_rows(
+                jnp.concatenate([v[0] for v in values], axis=0),
+                jnp.concatenate([v[1] for v in values], axis=0),
+            ),
+            matrix,
+        )
+        return [(y[8 * k : 8 * k + 8, :128], y[8 * k : 8 * k + 8, 128:]) for k in range(32)]
+
     stores = []
-    for group in range(4):
-        res, ims = [], []
-        for i in range(16 * group, 16 * group + 16, 2):
-            x = jnp.concatenate([raws[i], raws[i + 1]], axis=1)
-            xh, xl = split(x)
-            y = dot(first, jnp.concatenate([xh, xl], axis=0))
-            y = y[:64] + y[64:]
-            zr, zi = times(y[:32], y[32:], tr, ti)
-            res += [zr[:, :128], zr[:, 128:]]
-            ims += [zi[:, :128], zi[:, 128:]]
-        if group == 0:
-            for i in range(4, 10):
-                loads[i].wait()
-        second, third = mats[0:768, :], mats[768:1536, :]
-        last = mats[1536:1664, :][:, :128]
-        spectrum = dot(
-            left_rows(jnp.concatenate(res, axis=0), jnp.concatenate(ims, axis=0)), second
-        )
-        sr = spectrum[:, :128].reshape(16, 32, 128)
-        si = spectrum[:, 128:].reshape(16, 32, 128)
-        sr, si = times(sr, si, hr[None], hi[None])
-        back = dot(left_rows(sr.reshape(512, 128), si.reshape(512, 128)), third)
-        br = back[:, :128].reshape(16, 32, 128)
-        bi = back[:, 128:].reshape(16, 32, 128)
-        br, bi = times(br, bi, small[2][None], small[3][None])
-        for i in range(0, 16, 2):
-            cols = [jnp.concatenate([br[k], bi[k]], axis=0) for k in (i, i + 1)]
-            xh, xl = split(jnp.concatenate(cols, axis=1))
-            y = dot(last, jnp.concatenate([xh, xl], axis=0))
-            y = y[:64] + y[64:]
-            for k in range(2):
-                line, c = (i + k) // 4, (i + k) % 4
+    for half in range(2):
+        for c in range(4):
+            base = half * 8 * PITCH + c * 64
+            x = [
+                tuple(raws[pl.ds(base + 2 * t + part, 8, stride=PITCH), :] for part in range(2))
+                for t in range(32)
+            ]
+            x = apply(small_fft(x, -1), small[0], small[1])
+            if half == 0 and c == 0:
+                for copy in loads[10:]:
+                    copy.wait()
+            x = apply(lanes(x, mats[0:768, :]), hr, hi)
+            x = apply(lanes(x, mats[768:1536, :]), small[2], small[3])
+            for nt, value in enumerate(small_fft(x, 1)):
                 for part in range(2):
-                    kept[group % 2, c, pl.ds(part * 4 + line, 32, stride=8), :] = y[
-                        32 * part : 32 * part + 32, 128 * k : 128 * k + 128
-                    ]
-        if group % 2 == 0:
-            continue
-        half = group // 2
-        parts = [kept.at[g, c] for g in range(2) for c in range(4)]
+                    kept[nt, part * 4 + c] = value[part]
         for i in range(32):
-            blocks = swap_blocks([p[8 * i : 8 * i + 8, :] for p in parts])
+            blocks = swap_blocks([kept[i, e] for e in range(8)])
             for d, block in enumerate(blocks):
                 place = int(PLACE[4 * i + d // 2]) + 128 * (d % 2)
                 held[half, place] = block
@@ -260,13 +239,13 @@
         out_specs=anywhere,
         out_shape=jax.ShapeDtypeStruct((256, 16, 128), F32),
         scratch_shapes=[
-            pltpu.VMEM((64, 64, 128), F32),
+            pltpu.VMEM((16 * PITCH, 128), F32),
             pltpu.VMEM(matrices.shape, BF16),
             pltpu.VMEM((4, 32, 128), F32),
             pltpu.VMEM((64, 128), F32),
-            pltpu.VMEM((2, 4, 256, 128), F32),
+            pltpu.VMEM((32, 8, 8, 128), F32),
             pltpu.VMEM((2, 256, 8, 128), F32),
-            pltpu.SemaphoreType.DMA((10,)),
+            pltpu.SemaphoreType.DMA((19,)),
             pltpu.SemaphoreType.DMA((16,)),
         ],
         compiler_params=pltpu.CompilerParams(vmem_limit_bytes=RANGE_VMEM),
@@ -279,26 +258,19 @@
     low = lax.broadcasted_iota(jnp.int32, (128, 128), 1) < 64
     f = table[...]
     f = jnp.concatenate([f[:, :256], f], axis=1)
-    for half, line in itertools.product(range(2), range(4)):
-        cols = [
-            jnp.concatenate(
-                [turned[128 * s : 128 * s + 128, half * 8 + part * 4 + line, :] for s in range(2)], 1
-            )
-            for part in range(2)
-        ]
-        y = dot(f, right_cols(jnp.concatenate(cols, axis=0)))
-        pairs = []
-        for part in range(2):
-            a, b = y[128 * part : 128 * part + 128, :128], y[128 * part : 128 * part + 128, 128:]
+    for j in range(0, 16, 2):
+        cols = []
+        for line in (j, j + 1):
+            a, b = turned[0:128, line, :], turned[128:256, line, :]
             m = pltpu.roll(jnp.where(low, b, a), 64, 1)
-            pairs.append((jnp.where(low, a, m), jnp.where(low, m, b)))
+            cols.append(jnp.concatenate([jnp.where(low, a, m), jnp.where(low, m, b)], axis=0))
+        y = dot(f, right_cols(jnp.concatenate(cols, axis=1)))
         for k in range(2):
-            j = half * 8 + 4 * k + line
-            re, im = pairs[0][k], pairs[1][k]
-            if j:
-                re, im = times(re, im, twist[0, :, j : j + 1], twist[1, :, j : j + 1])
-            held[j, 0] = re
-            held[j, 1] = im
+            re, im = y[:128, 128 * k : 128 * k + 128], y[128:, 128 * k : 128 * k + 128]
+            if j + k:
+                re, im = times(re, im, twist[0, :, j + k : j + k + 1], twist[1, :, j + k : j + k + 1])
+            held[j + k, 0] = re
+            held[j + k, 1] = im
 
     low_core = ch[0] == 0
 
@@ -408,7 +380,7 @@
 def body(raw, range_filter, recon, rcmc_coef, band_offset, band_width, az_filter):
     ch = lax.axis_index("ch")
     blocks = lax.axis_size(BLK)
-    raw_rows = raw.reshape(16, 4, 2, 32, 128).transpose(0, 1, 3, 2, 4).reshape(64, 64, 128)
+    raw_rows = raw.reshape(16, 4, 2, 32, 128).transpose(0, 1, 3, 2, 4).reshape(4096, 128)
     filt_rows = range_filter.reshape(2, 32, 128).transpose(1, 0, 2).reshape(64, 128)
     pieces = compress(raw_rows, filt_rows)
     (pieces, recon, rcmc_coef, az_filter, band_offset) = lax.optimization_barrier(

time: 91.1 us -> 89.8 us (0.986)
  Pallas kernels: 12.8 us -> 11.4 us
    pallas_call x1, Pallas kernels: 7.99 us -> 6.75 us  [compress(): pl.pallas_call(range_kernel, in_specs=[anywhere] * 4, out_specs=anywhere,...]
where the time goes in v3:
time: 89.8 us; the launch traced here: 89.6 us
  waiting for transfers between devices  50.3 us (56%)
  starting transfers between devices  19.5 us (22%)
  Pallas kernels  11.4 us (13%)
  local copies, waits for them, and re-layouts  7.77 us (9%)
    all_to_all x1, waiting for transfers between devices, body(): lax.all_to_all(pieces, TURN, split_axis=0, concat_axis=0, tiled=True)  44.5 us
    all_to_all x1, starting transfers between devices, body(): lax.all_to_all(pieces, TURN, split_axis=0, concat_axis=0, tiled=True)  14.7 us
    pallas_call x1, Pallas kernels, compress(): pl.pallas_call(range_kernel, in_specs=[anywhere] * 4, out_specs=anywhere,...  6.75 us
    ppermute x1, waiting for transfers between devices, body(): far = lax.ppermute(far, EVERY, cross)  5.74 us
    ppermute x1, starting transfers between devices, body(): far = lax.ppermute(far, EVERY, cross)  4.75 us
    reshape x2, local copies, waits for them, and re-layouts, body(): az = az_filter.reshape(2, 128, 16, 16).transpose(0, 2, 3, 1)  4.23 us
    pallas_call x1, Pallas kernels, doppler_mix(): pl.pallas_call(mix_kernel, in_specs=[pl.BlockSpec(memory_space=pltpu.SMEM...  3.29 us
    reshape x2, local copies, waits for them, and re-layouts, body(): weights = recon.reshape(2, 8, 128, 16).transpose(0, 1, 3, 2)  2.86 us
  transfers between devices with their start and end apart: 3, of which 2 were waited for; matrix products, arithmetic and copies ran while one was open for 9% of the time, Pallas kernels for 0%

profile of v3, /device:TPU:2, one launch (start us, length us, event | category | flops | bytes accessed | tf_op | source)
XLA Modules:
  0.0 89.6 jit_solution(5008945016318895704)
XLA Ops:
  0.0 6.7 %range_compress.1 = f32[256,16,128]{2,1,0:T(8,128)} custom-call(f32[4096,128]{1,0:T(8,128)} %bitcast.24, f32[64,128]{1,0:T(8,128)} %bitcast.25, bf16[1536,256]{1,0:T(8,128)(2,1)} %constant.11.clone.matrices, f32[4,32,128]{2,1,0:T(8,128)} %constant.28.clone.twists), custom_call_target="tpu_custom_call" | custom-call | flops 4000000000 | bytes 4194304 | tf_op jit(solution)/shard_map/range_compress/pallas_call | solution.py:236
  6.8 14.7 %all-to-all-start = ((f32[256,16,128]{2,1,0:T(8,128)}), f32[256,16,128]{2,1,0:T(8,128)S(1)}, u32[]{:S(2)}, u32[]{:S(2)}) async-start(f32[256,16,128]{2,1,0:T(8,128)} %range_compress.1), calls=%async_computation | async-start | bytes 4194304 | tf_op jit(solution)/shard_map/all_to_all | solution.py:389
  21.5 1.3 %reshape.80 = f32[2,8,128,16]{3,2,1,0:T(8,128)} reshape(f32[2,8,2048]{2,1,0:T(8,128)S(1)} %copy-done.6) | data formatting | bytes 262144 | tf_op jit(solution)/shard_map/reshape | solution.py:390
  22.8 1.5 %copy.24 = f32[2,8,128,16]{2,3,1,0:T(8,128)S(1)} copy(f32[2,8,128,16]{3,2,1,0:T(8,128)} %reshape.80) | data formatting | bytes 262144 | tf_op jit(solution)/shard_map/reshape | solution.py:390
  24.4 0.2 reshape.81
  24.6 0.2 copy.25
  24.8 0.0 copy-start.8
  24.8 0.0 copy-start.3
  24.8 0.0 copy-start.4
  24.8 2.1 %reshape.82 = f32[2,128,16,16]{2,1,3,0:T(8,128)} reshape(f32[2,2048,16]{1,2,0:T(8,128)S(1)} %copy-done.5) | data formatting | bytes 524288 | tf_op jit(solution)/shard_map/reshape | solution.py:392
  26.9 2.2 %copy.26 = f32[2,128,16,16]{1,3,2,0:T(8,128)S(1)} copy(f32[2,128,16,16]{2,1,3,0:T(8,128)} %reshape.82) | data formatting | bytes 524288 | tf_op jit(solution)/shard_map/reshape | solution.py:392
  29.1 0.1 add.51
  29.2 0.1 add.53
  29.3 0.1 lt.19
  29.4 0.1 pad_add_fusion
  29.5 0.1 compare_and_fusion
  29.6 0.1 add_convert_fusion.select
  29.7 44.5 %all-to-all-done.turned = f32[256,16,128]{2,1,0:T(8,128)S(1)} async-done(((f32[256,16,128]{2,1,0:T(8,128)}), f32[256,16,128]{2,1,0:T(8,128)S(1)}, u32[]{:S(2)}, u32[]{:S(2)}) %all-to-all-start) | async-done | bytes 2097184 | tf_op jit(solution)/shard_map/all_to_all | solution.py:389
  74.2 0.0 copy-start
  74.2 3.3 %doppler_mix.1 = (f32[16,2,16,128]{3,2,1,0:T(8,128)S(1)}, f32[16,2,8,128]{3,2,1,0:T(8,128)S(1)}, f32[16,2,8,128]{3,2,1,0:T(8,128)S(1)}) custom-call(s32[1]{0:T(128)} %bitcast.ch, f32[256,16,128]{2,1,0:T(8,128)S(1)} %all-to-all-done.turned, bf16[256,512]{1,0:T(8,128)(2,1)S(1)} %copy-done.2, f32[2,128,16]{2,1,0:T(8,128)S(1)} %copy-done.3, ...), custom_call_target="tpu_custom_call" | custom-call | flops 4000000000 | bytes 4194304 | tf_op jit(solution)/shard_map/doppler_mix/pallas_call | solution.py:310
  77.5 0.1 collective-permute-start
  77.6 4.7 %collective-permute-start.1 = (f32[16,2,8,128]{3,2,1,0:T(8,128)S(1)}, f32[16,2,8,128]{3,2,1,0:T(8,128)S(1)}, u32[]{:S(2)}, u32[]{:S(2)}) collective-permute-start(f32[16,2,8,128]{3,2,1,0:T(8,128)S(1)} %get-tuple-element.27), channel_id=1, source_target_pairs={{1,2},{2,1},{3,4},{4,3},{5,6},{6,5},{7,8},{8,7},{9,10},{10,9},{11,... | collective-permute-start | bytes 393224 | tf_op jit(solution)/shard_map/ppermute | solution.py:402
  82.4 5.7 %collective-permute-done.1.far = f32[16,2,8,128]{3,2,1,0:T(8,128)S(1)} collective-permute-done((f32[16,2,8,128]{3,2,1,0:T(8,128)S(1)}, f32[16,2,8,128]{3,2,1,0:T(8,128)S(1)}, u32[]{:S(2)}, u32[]{:S(2)}) %collective-permute-start.1) | collective-permute-done | bytes 131104 | tf_op jit(solution)/shard_map/ppermute | solution.py:402
  88.2 1.4 %focus.1 = f32[2,16,2048]{2,1,0:T(8,128)} custom-call(f32[16,2,16,128]{3,2,1,0:T(8,128)S(1)} %get-tuple-element.25.own, f32[16,2,8,128]{3,2,1,0:T(8,128)S(1)} %collective-permute-done.near, f32[16,2,8,128]{3,2,1,0:T(8,128)S(1)} %collective-permute-done.1.far, bf16[128,64]{1,0:T(8,128)(2,1)S(1)} %add_convert_fusion.select, f32[8,16,128]{2,1,0:T(8,128)S(1)} %bitcast.22, ...), custom_call_target="tpu_custom_call" | custom-call | tf_op jit(solution)/shard_map/focus/pallas_call | solution.py:353
  (25 shorter events, 0.1 us)
Async XLA Ops:
  6.8 14.7 %copy-start.6 = (f32[2,8,2048]{2,1,0:T(8,128)S(1)}, f32[2,8,2048]{2,1,0:T(8,128)}, u32[]{:S(2)}) copy-start(f32[2,8,2048]{2,1,0:T(8,128)} %param.16) | copy-start | bytes 393220
  6.8 67.4 %all-to-all-start = ((f32[256,16,128]{2,1,0:T(8,128)}), f32[256,16,128]{2,1,0:T(8,128)S(1)}, u32[]{:S(2)}, u32[]{:S(2)}) async-start(f32[256,16,128]{2,1,0:T(8,128)} %range_compress.1), calls=%async_computation | async-start | bytes 4194304 | tf_op jit(solution)/shard_map/all_to_all | solution.py:389
  21.5 2.9 %copy-start.7 = (f32[8,2048]{1,0:T(8,128)S(1)}, f32[8,2048]{1,0:T(8,128)}, u32[]{:S(2)}) copy-start(f32[8,2048]{1,0:T(8,128)} %param.17) | copy-start | bytes 196612
  21.5 3.3 %copy-start.5 = (f32[2,2048,16]{1,2,0:T(8,128)S(1)}, f32[2,2048,16]{1,2,0:T(8,128)}, u32[]{:S(2)}) copy-start(f32[2,2048,16]{1,2,0:T(8,128)} %param.20) | copy-start | bytes 786436
  24.8 4.3 %copy-start.9 = (s32[16]{0:T(128)S(1)}, s32[16]{0:T(128)}, u32[]{:S(2)}) copy-start(s32[16]{0:T(128)} %param.18) | copy-start | bytes 196
  24.8 4.5 %copy-start.8 = (s32[16]{0:T(128)S(1)}, s32[16]{0:T(128)}, u32[]{:S(2)}) copy-start(s32[16]{0:T(128)} %param.19) | copy-start | bytes 196
  24.8 49.4 %copy-start.2 = (bf16[256,512]{1,0:T(8,128)(2,1)S(1)}, bf16[256,512]{1,0:T(8,128)(2,1)}, u32[]{:S(2)}) copy-start(bf16[256,512]{1,0:T(8,128)(2,1)} %constant.29.clone.table) | copy-start | bytes 786436
  24.8 49.4 %copy-start.3 = (f32[2,128,16]{2,1,0:T(8,128)S(1)}, f32[2,128,16]{2,1,0:T(8,128)}, u32[]{:S(2)}) copy-start(f32[2,128,16]{2,1,0:T(8,128)} %constant.30.clone.twist) | copy-start | bytes 49156
  24.8 49.4 %copy-start.4 = (bf16[128,256]{1,0:T(8,128)(2,1)S(1)}, bf16[128,256]{1,0:T(8,128)(2,1)}, u32[]{:S(2)}) copy-start(bf16[128,256]{1,0:T(8,128)(2,1)} %constant.31.clone.eye) | copy-start | bytes 196612
  74.2 13.9 %copy-start = (bf16[768,256]{1,0:T(8,128)(2,1)S(1)}, bf16[768,256]{1,0:T(8,128)(2,1)}, u32[]{:S(2)}) copy-start(bf16[768,256]{1,0:T(8,128)(2,1)} %constant.32.clone.right) | copy-start | bytes 1179652
  74.2 13.9 %copy-start.1 = (f32[2,16,128]{2,1,0:T(8,128)S(1)}, f32[2,16,128]{2,1,0:T(8,128)}, u32[]{:S(2)}) copy-start(f32[2,16,128]{2,1,0:T(8,128)} %constant.33.clone.twist) | copy-start | bytes 49156
  77.5 4.9 %collective-permute-start = (f32[16,2,8,128]{3,2,1,0:T(8,128)S(1)}, f32[16,2,8,128]{3,2,1,0:T(8,128)S(1)}, u32[]{:S(2)}, u32[]{:S(2)}) collective-permute-start(f32[16,2,8,128]{3,2,1,0:T(8,128)S(1)} %get-tuple-element.26), channel_id=1, source_target_pairs={{0,1},{1,0},{2,3},{3,2},{4,5},{5,4},{6,7},{7,6},{8,9},{9,8},{10,11... | collective-permute-start | bytes 393224 | tf_op jit(solution)/shard_map/ppermute | solution.py:403
  77.6 10.5 %collective-permute-start.1 = (f32[16,2,8,128]{3,2,1,0:T(8,128)S(1)}, f32[16,2,8,128]{3,2,1,0:T(8,128)S(1)}, u32[]{:S(2)}, u32[]{:S(2)}) collective-permute-start(f32[16,2,8,128]{3,2,1,0:T(8,128)S(1)} %get-tuple-element.27), channel_id=1, source_target_pairs={{1,2},{2,1},{3,4},{4,3},{5,6},{6,5},{7,8},{8,7},{9,10},{10,9},{11,... | collective-permute-start | bytes 393224 | tf_op jit(solution)/shard_map/ppermute | solution.py:402

commit v4 on v3

--- a/solution.py
+++ b/solution.py
@@ -261,7 +261,7 @@
     for j in range(0, 16, 2):
         cols = []
         for line in (j, j + 1):
-            a, b = turned[0:128, line, :], turned[128:256, line, :]
+            a, b = turned[pl.ds(line, 128, stride=16), :], turned[pl.ds(2048 + line, 128, stride=16), :]
             m = pltpu.roll(jnp.where(low, b, a), 64, 1)
             cols.append(jnp.concatenate([jnp.where(low, a, m), jnp.where(low, m, b)], axis=0))
         y = dot(f, right_cols(jnp.concatenate(cols, axis=1)))
@@ -316,7 +316,7 @@
         compiler_params=pltpu.CompilerParams(vmem_limit_bytes=24 * 2**20),
         cost_estimate=pl.CostEstimate(flops=4 * 10**9, bytes_accessed=2**22, transcendentals=0),
         name="doppler_mix",
-    )(ch, turned, table, twist, eye, weights)
+    )(ch, turned.reshape(4096, 128), table, twist, eye, weights)
 
 
 def focus_kernel(own, near, far, select, coef, az, right, twist, out, held):

time: 89.8 us -> 89.4 us (level)
  no operation moved by 1% of the time
where the time goes in v4:
time: 89.4 us; the launch traced here: 89.1 us
  waiting for transfers between devices  50.3 us (56%)
  starting transfers between devices  19.5 us (22%)
  Pallas kernels  11 us (12%)
  local copies, waits for them, and re-layouts  7.77 us (9%)
    all_to_all x1, waiting for transfers between devices, body(): lax.all_to_all(pieces, TURN, split_axis=0, concat_axis=0, tiled=True)  44.5 us
    all_to_all x1, starting transfers between devices, body(): lax.all_to_all(pieces, TURN, split_axis=0, concat_axis=0, tiled=True)  14.7 us
    pallas_call x1, Pallas kernels, compress(): pl.pallas_call(range_kernel, in_specs=[anywhere] * 4, out_specs=anywhere,...  6.75 us
    ppermute x1, waiting for transfers between devices, body(): far = lax.ppermute(far, EVERY, cross)  5.73 us
    ppermute x1, starting transfers between devices, body(): far = lax.ppermute(far, EVERY, cross)  4.75 us
    reshape x2, local copies, waits for them, and re-layouts, body(): az = az_filter.reshape(2, 128, 16, 16).transpose(0, 2, 3, 1)  4.23 us
    pallas_call x1, Pallas kernels, doppler_mix(): pl.pallas_call(mix_kernel, in_specs=[pl.BlockSpec(memory_space=pltpu.SMEM...  2.88 us
    reshape x2, local copies, waits for them, and re-layouts, body(): weights = recon.reshape(2, 8, 128, 16).transpose(0, 1, 3, 2)  2.86 us
  transfers between devices with their start and end apart: 3, of which 2 were waited for; matrix products, arithmetic and copies ran while one was open for 9% of the time, Pallas kernels for 0%

profile of v4, /device:TPU:2, one launch (start us, length us, event | category | flops | bytes accessed | tf_op | source)
XLA Modules:
  0.0 89.1 jit_solution(17193930496632114917)
XLA Ops:
  0.0 6.7 %range_compress.1 = f32[256,16,128]{2,1,0:T(8,128)} custom-call(f32[4096,128]{1,0:T(8,128)} %bitcast.26, f32[64,128]{1,0:T(8,128)} %bitcast.27, bf16[1536,256]{1,0:T(8,128)(2,1)} %constant.11.clone.matrices, f32[4,32,128]{2,1,0:T(8,128)} %constant.28.clone.twists), custom_call_target="tpu_custom_call" | custom-call | flops 4000000000 | bytes 4194304 | tf_op jit(solution)/shard_map/range_compress/pallas_call | solution.py:236
  6.8 14.7 %all-to-all-start = ((f32[256,16,128]{2,1,0:T(8,128)}), f32[256,16,128]{2,1,0:T(8,128)S(1)}, u32[]{:S(2)}, u32[]{:S(2)}) async-start(f32[256,16,128]{2,1,0:T(8,128)} %range_compress.1), calls=%async_computation | async-start | bytes 4194304 | tf_op jit(solution)/shard_map/all_to_all | solution.py:389
  21.5 1.3 %reshape.83 = f32[2,8,128,16]{3,2,1,0:T(8,128)} reshape(f32[2,8,2048]{2,1,0:T(8,128)S(1)} %copy-done.6) | data formatting | bytes 262144 | tf_op jit(solution)/shard_map/reshape | solution.py:390
  22.8 1.5 %copy.24 = f32[2,8,128,16]{2,3,1,0:T(8,128)S(1)} copy(f32[2,8,128,16]{3,2,1,0:T(8,128)} %reshape.83) | data formatting | bytes 262144 | tf_op jit(solution)/shard_map/reshape | solution.py:390
  24.4 0.2 reshape.84
  24.6 0.2 copy.25
  24.8 0.0 copy-start.8
  24.8 0.0 copy-start.3
  24.8 0.0 copy-start.4
  24.8 2.1 %reshape.85 = f32[2,128,16,16]{2,1,3,0:T(8,128)} reshape(f32[2,2048,16]{1,2,0:T(8,128)S(1)} %copy-done.5) | data formatting | bytes 524288 | tf_op jit(solution)/shard_map/reshape | solution.py:392
  26.9 2.2 %copy.26 = f32[2,128,16,16]{1,3,2,0:T(8,128)S(1)} copy(f32[2,128,16,16]{2,1,3,0:T(8,128)} %reshape.85) | data formatting | bytes 524288 | tf_op jit(solution)/shard_map/reshape | solution.py:392
  29.1 0.1 add.51
  29.2 0.1 add.53
  29.3 0.1 lt.19
  29.4 0.1 pad_add_fusion
  29.5 0.1 compare_and_fusion
  29.6 0.1 add_convert_fusion.select
  29.7 44.5 %all-to-all-done = f32[256,16,128]{2,1,0:T(8,128)S(1)} async-done(((f32[256,16,128]{2,1,0:T(8,128)}), f32[256,16,128]{2,1,0:T(8,128)S(1)}, u32[]{:S(2)}, u32[]{:S(2)}) %all-to-all-start) | async-done | bytes 2097184 | tf_op jit(solution)/shard_map/all_to_all | solution.py:389
  74.2 0.0 copy-start
  74.2 2.9 %doppler_mix.1 = (f32[16,2,16,128]{3,2,1,0:T(8,128)S(1)}, f32[16,2,8,128]{3,2,1,0:T(8,128)S(1)}, f32[16,2,8,128]{3,2,1,0:T(8,128)S(1)}) custom-call(s32[1]{0:T(128)} %bitcast.ch, f32[4096,128]{1,0:T(8,128)S(1)} %bitcast.22, bf16[256,512]{1,0:T(8,128)(2,1)S(1)} %copy-done.2, f32[2,128,16]{2,1,0:T(8,128)S(1)} %copy-done.3, bf16[128,256]{1,0:T(8,128)(2,1)S(1)} %copy-done.4, ...), custom_call_target="tpu_custom_call" | custom-call | flops 4000000000 | bytes 4194304 | tf_op jit(solution)/shard_map/doppler_mix/pallas_call | solution.py:310
  77.1 0.1 collective-permute-start
  77.2 4.8 %collective-permute-start.1 = (f32[16,2,8,128]{3,2,1,0:T(8,128)S(1)}, f32[16,2,8,128]{3,2,1,0:T(8,128)S(1)}, u32[]{:S(2)}, u32[]{:S(2)}) collective-permute-start(f32[16,2,8,128]{3,2,1,0:T(8,128)S(1)} %get-tuple-element.27), channel_id=1, source_target_pairs={{1,2},{2,1},{3,4},{4,3},{5,6},{6,5},{7,8},{8,7},{9,10},{10,9},{11,... | collective-permute-start | bytes 393224 | tf_op jit(solution)/shard_map/ppermute | solution.py:402
  82.0 5.7 %collective-permute-done.1.far = f32[16,2,8,128]{3,2,1,0:T(8,128)S(1)} collective-permute-done((f32[16,2,8,128]{3,2,1,0:T(8,128)S(1)}, f32[16,2,8,128]{3,2,1,0:T(8,128)S(1)}, u32[]{:S(2)}, u32[]{:S(2)}) %collective-permute-start.1) | collective-permute-done | bytes 131104 | tf_op jit(solution)/shard_map/ppermute | solution.py:402
  87.7 1.4 %focus.1 = f32[2,16,2048]{2,1,0:T(8,128)} custom-call(f32[16,2,16,128]{3,2,1,0:T(8,128)S(1)} %get-tuple-element.25.own, f32[16,2,8,128]{3,2,1,0:T(8,128)S(1)} %collective-permute-done.near, f32[16,2,8,128]{3,2,1,0:T(8,128)S(1)} %collective-permute-done.1.far, bf16[128,64]{1,0:T(8,128)(2,1)S(1)} %add_convert_fusion.select, f32[8,16,128]{2,1,0:T(8,128)S(1)} %bitcast.24, ...), custom_call_target="tpu_custom_call" | custom-call | tf_op jit(solution)/shard_map/focus/pallas_call | solution.py:353
  (25 shorter events, 0.1 us)
Async XLA Ops:
  6.8 14.7 %copy-start.6 = (f32[2,8,2048]{2,1,0:T(8,128)S(1)}, f32[2,8,2048]{2,1,0:T(8,128)}, u32[]{:S(2)}) copy-start(f32[2,8,2048]{2,1,0:T(8,128)} %param.16) | copy-start | bytes 393220
  6.8 67.4 %all-to-all-start = ((f32[256,16,128]{2,1,0:T(8,128)}), f32[256,16,128]{2,1,0:T(8,128)S(1)}, u32[]{:S(2)}, u32[]{:S(2)}) async-start(f32[256,16,128]{2,1,0:T(8,128)} %range_compress.1), calls=%async_computation | async-start | bytes 4194304 | tf_op jit(solution)/shard_map/all_to_all | solution.py:389
  21.5 2.9 %copy-start.7 = (f32[8,2048]{1,0:T(8,128)S(1)}, f32[8,2048]{1,0:T(8,128)}, u32[]{:S(2)}) copy-start(f32[8,2048]{1,0:T(8,128)} %param.17) | copy-start | bytes 196612
  21.5 3.3 %copy-start.5 = (f32[2,2048,16]{1,2,0:T(8,128)S(1)}, f32[2,2048,16]{1,2,0:T(8,128)}, u32[]{:S(2)}) copy-start(f32[2,2048,16]{1,2,0:T(8,128)} %param.20) | copy-start | bytes 786436
  24.8 4.3 %copy-start.9 = (s32[16]{0:T(128)S(1)}, s32[16]{0:T(128)}, u32[]{:S(2)}) copy-start(s32[16]{0:T(128)} %param.18) | copy-start | bytes 196
  24.8 4.5 %copy-start.8 = (s32[16]{0:T(128)S(1)}, s32[16]{0:T(128)}, u32[]{:S(2)}) copy-start(s32[16]{0:T(128)} %param.19) | copy-start | bytes 196
  24.8 49.4 %copy-start.2 = (bf16[256,512]{1,0:T(8,128)(2,1)S(1)}, bf16[256,512]{1,0:T(8,128)(2,1)}, u32[]{:S(2)}) copy-start(bf16[256,512]{1,0:T(8,128)(2,1)} %constant.29.clone.table) | copy-start | bytes 786436
  24.8 49.4 %copy-start.3 = (f32[2,128,16]{2,1,0:T(8,128)S(1)}, f32[2,128,16]{2,1,0:T(8,128)}, u32[]{:S(2)}) copy-start(f32[2,128,16]{2,1,0:T(8,128)} %constant.30.clone.twist) | copy-start | bytes 49156
  24.8 49.4 %copy-start.4 = (bf16[128,256]{1,0:T(8,128)(2,1)S(1)}, bf16[128,256]{1,0:T(8,128)(2,1)}, u32[]{:S(2)}) copy-start(bf16[128,256]{1,0:T(8,128)(2,1)} %constant.31.clone.eye) | copy-start | bytes 196612
  74.2 13.5 %copy-start = (bf16[768,256]{1,0:T(8,128)(2,1)S(1)}, bf16[768,256]{1,0:T(8,128)(2,1)}, u32[]{:S(2)}) copy-start(bf16[768,256]{1,0:T(8,128)(2,1)} %constant.32.clone.right) | copy-start | bytes 1179652
  74.2 13.5 %copy-start.1 = (f32[2,16,128]{2,1,0:T(8,128)S(1)}, f32[2,16,128]{2,1,0:T(8,128)}, u32[]{:S(2)}) copy-start(f32[2,16,128]{2,1,0:T(8,128)} %constant.33.clone.twist) | copy-start | bytes 49156
  77.1 4.9 %collective-permute-start = (f32[16,2,8,128]{3,2,1,0:T(8,128)S(1)}, f32[16,2,8,128]{3,2,1,0:T(8,128)S(1)}, u32[]{:S(2)}, u32[]{:S(2)}) collective-permute-start(f32[16,2,8,128]{3,2,1,0:T(8,128)S(1)} %get-tuple-element.26), channel_id=1, source_target_pairs={{0,1},{1,0},{2,3},{3,2},{4,5},{5,4},{6,7},{7,6},{8,9},{9,8},{10,11... | collective-permute-start | bytes 393224 | tf_op jit(solution)/shard_map/ppermute | solution.py:403
  77.2 10.5 %collective-permute-start.1 = (f32[16,2,8,128]{3,2,1,0:T(8,128)S(1)}, f32[16,2,8,128]{3,2,1,0:T(8,128)S(1)}, u32[]{:S(2)}, u32[]{:S(2)}) collective-permute-start(f32[16,2,8,128]{3,2,1,0:T(8,128)S(1)} %get-tuple-element.27), channel_id=1, source_target_pairs={{1,2},{2,1},{3,4},{4,3},{5,6},{6,5},{7,8},{8,7},{9,10},{10,9},{11,... | collective-permute-start | bytes 393224 | tf_op jit(solution)/shard_map/ppermute | solution.py:402

commit v5 on v4

--- a/solution.py
+++ b/solution.py
@@ -16,9 +16,9 @@
 RANGE_VMEM = 60 * 2**20
 UNROLL = 16
 PITCH = 264
-CHIP = np.arange(128).reshape(4, 4, 8).transpose(0, 2, 1).reshape(128)
+CHIP = np.arange(128).reshape(4, 4, 8).transpose(1, 2, 0).reshape(128)
 PLACE = np.argsort(CHIP)
-TURN = ("ch", "x", "z", "y")
+TURN = ("ch", "y", "z", "x")
 BLK = ("x", "y", "z")
 EVERY = ("x", "y", "z", "ch")
 
@@ -216,16 +216,11 @@
             for d, block in enumerate(blocks):
                 place = int(PLACE[4 * i + d // 2]) + 128 * (d % 2)
                 held[half, place] = block
-            if i % 8 == 7:
-                for core in range(2):
-                    spot = 128 * core + 4 * (i - 7)
-                    copy = pltpu.make_async_copy(
-                        held.at[half, spot : spot + 32],
-                        out.at[spot : spot + 32, 8 * half : 8 * half + 8, :],
-                        gone.at[len(stores)],
-                    )
-                    copy.start()
-                    stores.append(copy)
+        copy = pltpu.make_async_copy(
+            held.at[half], out.at[:, 8 * half : 8 * half + 8, :], gone.at[half]
+        )
+        copy.start()
+        stores.append(copy)
     for copy in stores:
         copy.wait()
 
@@ -246,7 +241,7 @@
             pltpu.VMEM((32, 8, 8, 128), F32),
             pltpu.VMEM((2, 256, 8, 128), F32),
             pltpu.SemaphoreType.DMA((19,)),
-            pltpu.SemaphoreType.DMA((16,)),
+            pltpu.SemaphoreType.DMA((2,)),
         ],
         compiler_params=pltpu.CompilerParams(vmem_limit_bytes=RANGE_VMEM),
         cost_estimate=pl.CostEstimate(flops=4 * 10**9, bytes_accessed=2**22, transcendentals=0),

time: 89.4 us -> 88.3 us (0.988)
  waiting for transfers between devices: 50.3 us -> 47.5 us
  starting transfers between devices: 19.5 us -> 21.3 us
    ppermute x1, starting transfers between devices: 4.75 us -> 6.5 us  [body(): far = lax.ppermute(far, EVERY, cross)]
    ppermute x1, waiting for transfers between devices: 5.73 us -> 3.99 us  [body(): far = lax.ppermute(far, EVERY, cross)]
    all_to_all x1, waiting for transfers between devices: 44.5 us -> 43.5 us  [body(): lax.all_to_all(pieces, TURN, split_axis=0, concat_axis=0, tiled=True)]
where the time goes in v5:
time: 88.3 us; the launch traced here: 88 us
  waiting for transfers between devices  47.5 us (54%)
  starting transfers between devices  21.3 us (24%)
  Pallas kernels  10.9 us (12%)
  local copies, waits for them, and re-layouts  7.77 us (9%)
    all_to_all x1, waiting for transfers between devices, body(): lax.all_to_all(pieces, TURN, split_axis=0, concat_axis=0, tiled=True)  43.5 us
    all_to_all x1, starting transfers between devices, body(): lax.all_to_all(pieces, TURN, split_axis=0, concat_axis=0, tiled=True)  14.7 us
    pallas_call x1, Pallas kernels, compress(): pl.pallas_call(range_kernel, in_specs=[anywhere] * 4, out_specs=anywhere,...  6.63 us
    ppermute x1, starting transfers between devices, body(): far = lax.ppermute(far, EVERY, cross)  6.5 us
    reshape x2, local copies, waits for them, and re-layouts, body(): az = az_filter.reshape(2, 128, 16, 16).transpose(0, 2, 3, 1)  4.23 us
    ppermute x1, waiting for transfers between devices, body(): far = lax.ppermute(far, EVERY, cross)  3.99 us
    pallas_call x1, Pallas kernels, doppler_mix(): pl.pallas_call(mix_kernel, in_specs=[pl.BlockSpec(memory_space=pltpu.SMEM...  2.88 us
    reshape x2, local copies, waits for them, and re-layouts, body(): weights = recon.reshape(2, 8, 128, 16).transpose(0, 1, 3, 2)  2.86 us
  transfers between devices with their start and end apart: 3, of which 2 were waited for; matrix products, arithmetic and copies ran while one was open for 9% of the time, Pallas kernels for 0%

profile of v5, /device:TPU:2, one launch (start us, length us, event | category | flops | bytes accessed | tf_op | source)
XLA Modules:
  0.0 88.0 jit_solution(8930582297660573748)
XLA Ops:
  0.0 6.6 %range_compress.1 = f32[256,16,128]{2,1,0:T(8,128)} custom-call(f32[4096,128]{1,0:T(8,128)} %bitcast.26, f32[64,128]{1,0:T(8,128)} %bitcast.27, bf16[1536,256]{1,0:T(8,128)(2,1)} %constant.11.clone.matrices, f32[4,32,128]{2,1,0:T(8,128)} %constant.28.clone.twists), custom_call_target="tpu_custom_call" | custom-call | flops 4000000000 | bytes 4194304 | tf_op jit(solution)/shard_map/range_compress/pallas_call | solution.py:231
  6.7 14.7 %all-to-all-start = ((f32[256,16,128]{2,1,0:T(8,128)}), f32[256,16,128]{2,1,0:T(8,128)S(1)}, u32[]{:S(2)}, u32[]{:S(2)}) async-start(f32[256,16,128]{2,1,0:T(8,128)} %range_compress.1), calls=%async_computation | async-start | bytes 4194304 | tf_op jit(solution)/shard_map/all_to_all | solution.py:384
  21.4 1.3 %reshape.83 = f32[2,8,128,16]{3,2,1,0:T(8,128)} reshape(f32[2,8,2048]{2,1,0:T(8,128)S(1)} %copy-done.6) | data formatting | bytes 262144 | tf_op jit(solution)/shard_map/reshape | solution.py:385
  22.7 1.5 %copy.24 = f32[2,8,128,16]{2,3,1,0:T(8,128)S(1)} copy(f32[2,8,128,16]{3,2,1,0:T(8,128)} %reshape.83) | data formatting | bytes 262144 | tf_op jit(solution)/shard_map/reshape | solution.py:385
  24.3 0.2 reshape.84
  24.5 0.2 copy.25
  24.6 0.0 copy-start.8
  24.7 0.0 copy-start.2
  24.7 0.0 copy-start.3
  24.7 0.0 copy-start.4
  24.7 2.1 %reshape.85 = f32[2,128,16,16]{2,1,3,0:T(8,128)} reshape(f32[2,2048,16]{1,2,0:T(8,128)S(1)} %copy-done.5) | data formatting | bytes 524288 | tf_op jit(solution)/shard_map/reshape | solution.py:387
  26.7 2.2 %copy.26 = f32[2,128,16,16]{1,3,2,0:T(8,128)S(1)} copy(f32[2,128,16,16]{2,1,3,0:T(8,128)} %reshape.85) | data formatting | bytes 524288 | tf_op jit(solution)/shard_map/reshape | solution.py:387
  29.0 0.1 add.51
  29.0 0.1 add.53
  29.1 0.1 lt.19
  29.3 0.1 pad_add_fusion
  29.3 0.1 compare_and_fusion
  29.4 0.1 add_convert_fusion.select
  29.5 43.5 %all-to-all-done = f32[256,16,128]{2,1,0:T(8,128)S(1)} async-done(((f32[256,16,128]{2,1,0:T(8,128)}), f32[256,16,128]{2,1,0:T(8,128)S(1)}, u32[]{:S(2)}, u32[]{:S(2)}) %all-to-all-start) | async-done | bytes 2097184 | tf_op jit(solution)/shard_map/all_to_all | solution.py:384
  73.1 2.9 %doppler_mix.1 = (f32[16,2,16,128]{3,2,1,0:T(8,128)S(1)}, f32[16,2,8,128]{3,2,1,0:T(8,128)S(1)}, f32[16,2,8,128]{3,2,1,0:T(8,128)S(1)}) custom-call(s32[1]{0:T(128)} %bitcast.ch, f32[4096,128]{1,0:T(8,128)S(1)} %bitcast.22, bf16[256,512]{1,0:T(8,128)(2,1)S(1)} %copy-done.2, f32[2,128,16]{2,1,0:T(8,128)S(1)} %copy-done.3, bf16[128,256]{1,0:T(8,128)(2,1)S(1)} %copy-done.4, ...), custom_call_target="tpu_custom_call" | custom-call | flops 4000000000 | bytes 4194304 | tf_op jit(solution)/shard_map/doppler_mix/pallas_call | solution.py:305
  76.0 0.1 collective-permute-start
  76.1 6.5 %collective-permute-start.1 = (f32[16,2,8,128]{3,2,1,0:T(8,128)S(1)}, f32[16,2,8,128]{3,2,1,0:T(8,128)S(1)}, u32[]{:S(2)}, u32[]{:S(2)}) collective-permute-start(f32[16,2,8,128]{3,2,1,0:T(8,128)S(1)} %get-tuple-element.27), channel_id=1, source_target_pairs={{1,2},{2,1},{3,4},{4,3},{5,6},{6,5},{7,8},{8,7},{9,10},{10,9},{11,... | collective-permute-start | bytes 393224 | tf_op jit(solution)/shard_map/ppermute | solution.py:397
  82.6 4.0 %collective-permute-done.1.far = f32[16,2,8,128]{3,2,1,0:T(8,128)S(1)} collective-permute-done((f32[16,2,8,128]{3,2,1,0:T(8,128)S(1)}, f32[16,2,8,128]{3,2,1,0:T(8,128)S(1)}, u32[]{:S(2)}, u32[]{:S(2)}) %collective-permute-start.1) | collective-permute-done | bytes 131104 | tf_op jit(solution)/shard_map/ppermute | solution.py:397
  86.6 1.4 %focus.1 = f32[2,16,2048]{2,1,0:T(8,128)} custom-call(f32[16,2,16,128]{3,2,1,0:T(8,128)S(1)} %get-tuple-element.25.own, f32[16,2,8,128]{3,2,1,0:T(8,128)S(1)} %collective-permute-done.near, f32[16,2,8,128]{3,2,1,0:T(8,128)S(1)} %collective-permute-done.1.far, bf16[128,64]{1,0:T(8,128)(2,1)S(1)} %add_convert_fusion.select, f32[8,16,128]{2,1,0:T(8,128)S(1)} %bitcast.24, ...), custom_call_target="tpu_custom_call" | custom-call | tf_op jit(solution)/shard_map/focus/pallas_call | solution.py:348
  (25 shorter events, 0.1 us)
Async XLA Ops:
  6.6 14.7 %copy-start.6 = (f32[2,8,2048]{2,1,0:T(8,128)S(1)}, f32[2,8,2048]{2,1,0:T(8,128)}, u32[]{:S(2)}) copy-start(f32[2,8,2048]{2,1,0:T(8,128)} %param.16) | copy-start | bytes 393220
  6.7 66.4 %all-to-all-start = ((f32[256,16,128]{2,1,0:T(8,128)}), f32[256,16,128]{2,1,0:T(8,128)S(1)}, u32[]{:S(2)}, u32[]{:S(2)}) async-start(f32[256,16,128]{2,1,0:T(8,128)} %range_compress.1), calls=%async_computation | async-start | bytes 4194304 | tf_op jit(solution)/shard_map/all_to_all | solution.py:384
  21.4 2.9 %copy-start.7 = (f32[8,2048]{1,0:T(8,128)S(1)}, f32[8,2048]{1,0:T(8,128)}, u32[]{:S(2)}) copy-start(f32[8,2048]{1,0:T(8,128)} %param.17) | copy-start | bytes 196612
  21.4 3.3 %copy-start.5 = (f32[2,2048,16]{1,2,0:T(8,128)S(1)}, f32[2,2048,16]{1,2,0:T(8,128)}, u32[]{:S(2)}) copy-start(f32[2,2048,16]{1,2,0:T(8,128)} %param.20) | copy-start | bytes 786436
  24.6 4.3 %copy-start.9 = (s32[16]{0:T(128)S(1)}, s32[16]{0:T(128)}, u32[]{:S(2)}) copy-start(s32[16]{0:T(128)} %param.18) | copy-start | bytes 196
  24.6 4.5 %copy-start.8 = (s32[16]{0:T(128)S(1)}, s32[16]{0:T(128)}, u32[]{:S(2)}) copy-start(s32[16]{0:T(128)} %param.19) | copy-start | bytes 196
  24.7 48.4 %copy-start.2 = (bf16[256,512]{1,0:T(8,128)(2,1)S(1)}, bf16[256,512]{1,0:T(8,128)(2,1)}, u32[]{:S(2)}) copy-start(bf16[256,512]{1,0:T(8,128)(2,1)} %constant.29.clone.table) | copy-start | bytes 786436
  24.7 48.4 %copy-start.3 = (f32[2,128,16]{2,1,0:T(8,128)S(1)}, f32[2,128,16]{2,1,0:T(8,128)}, u32[]{:S(2)}) copy-start(f32[2,128,16]{2,1,0:T(8,128)} %constant.30.clone.twist) | copy-start | bytes 49156
  24.7 48.4 %copy-start.4 = (bf16[128,256]{1,0:T(8,128)(2,1)S(1)}, bf16[128,256]{1,0:T(8,128)(2,1)}, u32[]{:S(2)}) copy-start(bf16[128,256]{1,0:T(8,128)(2,1)} %constant.31.clone.eye) | copy-start | bytes 196612
  73.1 13.5 %copy-start = (bf16[768,256]{1,0:T(8,128)(2,1)S(1)}, bf16[768,256]{1,0:T(8,128)(2,1)}, u32[]{:S(2)}) copy-start(bf16[768,256]{1,0:T(8,128)(2,1)} %constant.32.clone.right) | copy-start | bytes 1179652
  73.1 13.5 %copy-start.1 = (f32[2,16,128]{2,1,0:T(8,128)S(1)}, f32[2,16,128]{2,1,0:T(8,128)}, u32[]{:S(2)}) copy-start(f32[2,16,128]{2,1,0:T(8,128)} %constant.33.clone.twist) | copy-start | bytes 49156
  76.0 6.6 %collective-permute-start = (f32[16,2,8,128]{3,2,1,0:T(8,128)S(1)}, f32[16,2,8,128]{3,2,1,0:T(8,128)S(1)}, u32[]{:S(2)}, u32[]{:S(2)}) collective-permute-start(f32[16,2,8,128]{3,2,1,0:T(8,128)S(1)} %get-tuple-element.26), channel_id=1, source_target_pairs={{0,1},{1,0},{2,3},{3,2},{4,5},{5,4},{6,7},{7,6},{8,9},{9,8},{10,11... | collective-permute-start | bytes 393224 | tf_op jit(solution)/shard_map/ppermute | solution.py:398
  76.1 10.5 %collective-permute-start.1 = (f32[16,2,8,128]{3,2,1,0:T(8,128)S(1)}, f32[16,2,8,128]{3,2,1,0:T(8,128)S(1)}, u32[]{:S(2)}, u32[]{:S(2)}) collective-permute-start(f32[16,2,8,128]{3,2,1,0:T(8,128)S(1)} %get-tuple-element.27), channel_id=1, source_target_pairs={{1,2},{2,1},{3,4},{4,3},{5,6},{6,5},{7,8},{8,7},{9,10},{10,9},{11,... | collective-permute-start | bytes 393224 | tf_op jit(solution)/shard_map/ppermute | solution.py:397
